TPU v7x, 32 devices: a whole 2x2x4 slice. The times are simulated.
32 devices in a mesh: ctx: 8 (over z, x), tp: 4 (over y, core).
Axes of the slice: x: 2, y: 2, z: 4, core: 2. Of those that a mesh axis runs over, the one named last changes fastest.
Arguments:
- ssm_input: bfloat16 [4096, 16384], P('ctx', 'tp'), may hold values from -6 to 6
- gate_input: bfloat16 [4096, 16384], P('ctx', 'tp'), may hold values from -6 to 6
- state_maps: bfloat16 [4096, 2, 1024], P('ctx', None, 'tp'), may hold values from -6 to 6
- step_size: float32 [4096, 256], P('ctx', 'tp'), may hold values from 0 to 8, as said below
- decay_rate: float32 [256], P('tp'), may hold values from 0 to 1, as said below
- skip_gain: float32 [256], P('tp'), may hold values from 0.5 to 1.5
- conv_weight: float32 [4, 16384], P(None, 'tp'), may hold values from -0.5 to 0.5
- conv_bias: float32 [16384], P('tp'), may hold values from -0.5 to 0.5
- map_conv: float32 [4, 2, 1024], P(None, None, 'tp'), may hold values from -0.5 to 0.5
- map_bias: float32 [2, 1024], P(None, 'tp'), may hold values from -1 to 1
- norm_gain: float32 [16384], P('tp'), may hold values from 0.1 to 1.9
- out_weight: bfloat16 [16384, 4096], P('tp'), may hold values from -0.046875 to 0.046875
Outputs:
- mixer_out: bfloat16 [4096, 4096], P(('ctx', 'tp'))
Inputs may be any that keep to these rules, and one draw needn't show every extreme that they name: `step_size`: positive step of every token and head. `decay_rate`: positive rate of every head.
All inputs are finite; a program needn't handle non-finite values.
Results may differ from a plain program's by a relative error of at most 0.03.
Values may be sent and summed in bfloat16 or wider, within the bound.
A program may use at most 192 MiB of HBM per device.

v0:
```python
import jax
import jax.numpy as jnp
from jax import lax
from jax.sharding import PartitionSpec as P

HEAD_DIM = 64
STATE = 128
CONV = 4
BLOCK = 128


def passed_along(value, axis, steps):
    count = lax.axis_size(axis)
    first, last = (max(0, -steps), min(count, count - steps))
    return lax.ppermute(value, axis, [(source, source + steps) for source in range(first, last)])


def carried_in(value, axis, join, neutral):
    place = lax.axis_index(axis)
    gathered = jax.tree.map(
        lambda a, kind: lax.all_gather(a.astype(kind), axis), value, (jnp.bfloat16, jnp.bfloat16)
    )
    state = jax.tree.map(lambda a, e: jnp.zeros_like(a) + jnp.asarray(e, a.dtype), value, neutral)

    def one(step, state):
        return join(
            state,
            jax.tree.map(
                lambda a, own: lax.dynamic_index_in_dim(a, step, 0, False).astype(own.dtype),
                gathered,
                value,
            ),
        )

    return lax.fori_loop(0, place, one, state)


def causal_conv(values, lead_rows, weight, bias_term):
    padded = jnp.concatenate([lead_rows, values], axis=0)
    length = values.shape[0]
    accum = jnp.zeros(values.shape, jnp.float32) + bias_term
    for offset in range(weight.shape[0]):
        accum = accum + weight[offset] * padded[offset : offset + length].astype(jnp.float32)
    return jax.nn.silu(accum).astype(jnp.bfloat16)


def local(
    ssm_input,
    gate_input,
    state_maps,
    step_size,
    decay_rate,
    skip_gain,
    conv_weight,
    conv_bias,
    map_conv,
    map_bias,
    norm_gain,
    out_weight,
):
    length = ssm_input.shape[0]
    head_count = step_size.shape[1]
    inner_width = ssm_input.shape[1]
    groups = state_maps.shape[2] // STATE
    repeat = head_count // groups
    blocks = length // BLOCK
    lead_input, lead_maps = passed_along(
        (ssm_input[length - CONV + 1 :], state_maps[length - CONV + 1 :]), "ctx", 1
    )
    conv_out = causal_conv(ssm_input, lead_input, conv_weight, conv_bias)
    maps_out = causal_conv(state_maps, lead_maps, map_conv, map_bias)
    log_decay = -decay_rate[None, :] * step_size
    running = jnp.cumsum(log_decay.reshape(blocks, BLOCK, head_count), axis=1)
    values = conv_out.reshape(blocks, BLOCK, head_count, HEAD_DIM)
    input_maps = maps_out[:, 0].reshape(blocks, BLOCK, groups, STATE)
    output_maps = maps_out[:, 1].reshape(blocks, BLOCK, groups, STATE)
    block_steps = step_size.reshape(blocks, BLOCK, head_count)
    scores = jnp.einsum(
        "cqgn,csgn->cgqs", output_maps, input_maps, preferred_element_type=jnp.float32
    )
    scores = jnp.broadcast_to(scores[:, :, None], (blocks, groups, repeat, BLOCK, BLOCK)).reshape(
        blocks, head_count, BLOCK, BLOCK
    )
    head_major = jnp.transpose(running, (0, 2, 1))
    gap_log = head_major[:, :, :, None] - head_major[:, :, None, :]
    causal_mask = jnp.tril(jnp.ones((BLOCK, BLOCK), dtype=bool))
    decays = jnp.exp(jnp.where(causal_mask[None, None], gap_log, -1e30))
    step_major = jnp.transpose(block_steps, (0, 2, 1))
    weights = (scores * decays * step_major[:, :, None, :]).astype(jnp.bfloat16)
    within = jnp.einsum("chqs,cshp->cqhp", weights, values, preferred_element_type=jnp.float32)
    to_end = jnp.exp(running[:, -1:, :] - running) * block_steps
    input_heads = jnp.broadcast_to(
        input_maps[:, :, :, None], (blocks, BLOCK, groups, repeat, STATE)
    ).reshape(blocks, BLOCK, head_count, STATE)
    loaded = (input_heads.astype(jnp.float32) * to_end[..., None]).astype(jnp.bfloat16)
    fresh_state = jnp.einsum("cshn,cshp->chnp", loaded, values, preferred_element_type=jnp.float32)
    totals = running[:, -1, :]

    def advance(carry_state, inputs_pair):
        block_total, new_part = inputs_pair
        return (jnp.exp(block_total)[:, None, None] * carry_state + new_part, carry_state)

    empty_state = jnp.zeros((head_count, STATE, HEAD_DIM), jnp.float32)
    local_end, local_enter = lax.scan(advance, empty_state, (totals, fresh_state))
    device_log = jnp.sum(totals, axis=0)

    def combine(earlier, latter):
        return (earlier[0] + latter[0], jnp.exp(latter[0])[:, None, None] * earlier[1] + latter[1])

    empty_log = jnp.zeros((head_count,), jnp.float32)
    before_log, incoming = carried_in(
        (device_log, local_end), "ctx", combine, (empty_log, empty_state)
    )
    prior_log = jnp.cumsum(totals, axis=0) - totals
    entering = jnp.exp(prior_log)[:, :, None, None] * incoming[None] + local_enter
    carried = entering.astype(jnp.bfloat16).reshape(blocks, groups, repeat, STATE, HEAD_DIM)
    before = jnp.einsum(
        "cqgn,cgrnp->cqgrp", output_maps, carried, preferred_element_type=jnp.float32
    )
    before = jnp.exp(running)[..., None] * before.reshape(blocks, BLOCK, head_count, HEAD_DIM)
    output = within + before + skip_gain[None, None, :, None] * values.astype(jnp.float32)
    gated = output.reshape(length, inner_width) * jax.nn.silu(gate_input.astype(jnp.float32))
    grouped = gated.reshape(length, groups, inner_width // groups)
    inverse_rms = lax.rsqrt(jnp.mean(grouped * grouped, axis=2, keepdims=True) + 1e-05)
    normed = ((grouped * inverse_rms).reshape(length, inner_width) * norm_gain[None, :]).astype(
        jnp.bfloat16
    )
    return lax.psum_scatter(
        jnp.dot(normed, out_weight, preferred_element_type=jnp.float32).astype(jnp.bfloat16),
        "tp",
        scatter_dimension=0,
        tiled=True,
    )


def solution(mesh):
    in_specs = (
        P("ctx", "tp"),
        P("ctx", "tp"),
        P("ctx", None, "tp"),
        P("ctx", "tp"),
        P("tp"),
        P("tp"),
        P(None, "tp"),
        P("tp"),
        P(None, None, "tp"),
        P(None, "tp"),
        P("tp"),
        P("tp", None),
    )
    out_specs = P(("ctx", "tp"), None)
    return jax.shard_map(local, mesh=mesh, in_specs=in_specs, out_specs=out_specs, check_vma=False)
```

profile of v0, /device:TPU:26, one launch (start us, length us, event | category | flops | bytes accessed | tf_op | source)
XLA Modules:
  0.0 423.5 jit_solution(3568428244588914796)
XLA Ops:
  15.7 6.5 %copy.44 = bf16[512,4096]{0,1:T(8,128)(2,1)} copy(bf16[512,4096]{1,0:T(8,128)(2,1)} %param.16) | data formatting | bytes 8388608 | tf_op args[0]
  28.1 15.8 %multiply_convert_fusion.4 = bf16[512,4096]{0,1:T(8,128)(2,1)} fusion(bf16[512,4096]{0,1:T(8,128)(2,1)} %copy.44, bf16[3,4096]{0,1:T(8,128)(2,1)S(1)} %copy.43, f32[4096]{0:T(1024)S(1)} %bitcast.89, f32[4096]{0:T(1024)S(1)} %bitcast.90, f32[4096]{0:T(1024)S(1)} %bitcast.88, f32[4096]{0:T(1024)S(1)} %bitcast.87, f32[4096]{0:T(1024)S(1)} %copy-done.5), kind=kLoop, calls=%fused_computation.30 | loop fusion | flops 54525952 | bytes 8495104 | tf_op jit(solution)/shard_map/convert_element_type | solution.py:44
  44.0 6.9 %reshape.103 = bf16[4,128,64,64]{1,0,3,2:T(4,128)(2,1)} reshape(bf16[512,4096]{0,1:T(8,128)(2,1)} %multiply_convert_fusion.4) | data formatting | bytes 8388608 | tf_op jit(solution)/shard_map/reshape | solution.py:74
  50.9 7.8 %broadcast_in_dim.33 = f32[4,128,2,32,128]{4,1,3,2,0:T(8,128)} broadcast(f32[4,128,2,128]{3,1,2,0:T(8,128)S(1)} %copy.55), dimensions={0,1,2,4} | broadcast | bytes 17301504 | tf_op jit(solution)/shard_map/broadcast_in_dim | solution.py:92
  58.7 15.9 %fusion.7 = f32[4,64,128,64]{3,2,1,0:T(8,128)} fusion(f32[4,128,64,128]{3,1,2,0:T(8,128)} %bitcast.77, f32[4,128,64]{1,2,0:T(8,128)S(1)} %copy.56, bf16[4,128,64,64]{1,0,3,2:T(4,128)(2,1)S(1)} %copy-done.2), kind=kOutput, calls=%fused_computation.18 | convolution fusion | flops 545259520 | bytes 29491200 | tf_op jit(solution)/shard_map/cshn,cshp->chnp/dot_general | solution.py:96
  74.6 38.9 %while.26 = (s32[]{:T(128)}, f32[64,128,64]{2,1,0:T(8,128)}, f32[4,64,128,64]{3,2,1,0:T(8,128)}, f32[4,64]{1,0:T(4,128)S(1)}, f32[4,64,128,64]{3,2,1,0:T(8,128)}, /*index=5*/s32[]{:T(128)}, s32[]{:T(128)}) while((s32[]{:T(128)}, f32[64,128,64]{2,1,0:T(8,128)}, f32[4,64,128,64]{3,2,1,0:T(8,128)}, f32[4,64]{1,0:T(4,128)S(1)}, ...), condition=%wide.region_4.5_spmd.clone, body=%wide.region_3.4_spmd.clone.sunk | while | flops 2097155 | bytes 14681440 | solution.py:104
  77.1 4.6 %bitcast_add_fusion.3 = f32[64,128,64]{2,1,0:T(8,128)} fusion(f32[4,64,128,64]{3,2,1,0:T(8,128)} %get-tuple-element.233, s32[]{:T(128)} %get-tuple-element.222, f32[64,128,64]{2,1,0:T(8,128)} %get-tuple-element.223, f32[64]{0:T(128)S(1)} %fusion.34, pred[]{:T(512)S(6)} %compare.3), kind=kLoop, calls=%fused_computation.4.clone.1 | loop fusion | flops 1572864 | bytes 6291717 | tf_op jit(solution)/shard_map/while/body/eval_jaxpr/add | solution.py:101
  81.8 4.7 %bitcast_dynamic-update-slice_fusion.2 = f32[4,64,128,64]{3,2,1,0:T(8,128)} fusion(f32[4,64,128,64]{3,2,1,0:T(8,128)} %get-tuple-element.224, s32[]{:T(128)} %get-tuple-element.222, f32[64,128,64]{2,1,0:T(8,128)} %get-tuple-element.223, pred[]{:T(512)S(6)} %compare.3), kind=kLoop, calls=%fused_computation.3.clone.1 | loop fusion | flops 524288 | bytes 8389121 | tf_op jit(solution)/shard_map/while/body/jit(dynamic_update_index_in_dim)/dynamic_update_slice | solution.py:104
  86.5 5.9 %bitcast_add_fusion.3 = f32[64,128,64]{2,1,0:T(8,128)} fusion(f32[4,64,128,64]{3,2,1,0:T(8,128)} %get-tuple-element.233, s32[]{:T(128)} %get-tuple-element.222, f32[64,128,64]{2,1,0:T(8,128)} %get-tuple-element.223, f32[64]{0:T(128)S(1)} %fusion.34, pred[]{:T(512)S(6)} %compare.3), kind=kLoop, calls=%fused_computation.4.clone.1 | loop fusion | flops 1572864 | bytes 6291717 | tf_op jit(solution)/shard_map/while/body/eval_jaxpr/add | solution.py:101
  92.4 4.7 %bitcast_dynamic-update-slice_fusion.2 = f32[4,64,128,64]{3,2,1,0:T(8,128)} fusion(f32[4,64,128,64]{3,2,1,0:T(8,128)} %get-tuple-element.224, s32[]{:T(128)} %get-tuple-element.222, f32[64,128,64]{2,1,0:T(8,128)} %get-tuple-element.223, pred[]{:T(512)S(6)} %compare.3), kind=kLoop, calls=%fused_computation.3.clone.1 | loop fusion | flops 524288 | bytes 8389121 | tf_op jit(solution)/shard_map/while/body/jit(dynamic_update_index_in_dim)/dynamic_update_slice | solution.py:104
  97.1 5.9 %bitcast_add_fusion.3 = f32[64,128,64]{2,1,0:T(8,128)} fusion(f32[4,64,128,64]{3,2,1,0:T(8,128)} %get-tuple-element.233, s32[]{:T(128)} %get-tuple-element.222, f32[64,128,64]{2,1,0:T(8,128)} %get-tuple-element.223, f32[64]{0:T(128)S(1)} %fusion.34, pred[]{:T(512)S(6)} %compare.3), kind=kLoop, calls=%fused_computation.4.clone.1 | loop fusion | flops 1572864 | bytes 6291717 | tf_op jit(solution)/shard_map/while/body/eval_jaxpr/add | solution.py:101
  103.0 4.7 %bitcast_dynamic-update-slice_fusion.2 = f32[4,64,128,64]{3,2,1,0:T(8,128)} fusion(f32[4,64,128,64]{3,2,1,0:T(8,128)} %get-tuple-element.224, s32[]{:T(128)} %get-tuple-element.222, f32[64,128,64]{2,1,0:T(8,128)} %get-tuple-element.223, pred[]{:T(512)S(6)} %compare.3), kind=kLoop, calls=%fused_computation.3.clone.1 | loop fusion | flops 524288 | bytes 8389121 | tf_op jit(solution)/shard_map/while/body/jit(dynamic_update_index_in_dim)/dynamic_update_slice | solution.py:104
  107.7 5.9 %bitcast_add_fusion.3 = f32[64,128,64]{2,1,0:T(8,128)} fusion(f32[4,64,128,64]{3,2,1,0:T(8,128)} %get-tuple-element.233, s32[]{:T(128)} %get-tuple-element.222, f32[64,128,64]{2,1,0:T(8,128)} %get-tuple-element.223, f32[64]{0:T(128)S(1)} %fusion.34, pred[]{:T(512)S(6)} %compare.3), kind=kLoop, calls=%fused_computation.4.clone.1 | loop fusion | flops 1572864 | bytes 6291717 | tf_op jit(solution)/shard_map/while/body/eval_jaxpr/add | solution.py:101
  113.6 3.3 copy.59
  118.8 19.0 %all-reduce = bf16[512]{0:T(512)(128)(2,1)S(1)} all-reduce(bf16[512]{0:T(512)(128)(2,1)S(1)} %dynamic-update-slice), channel_id=2, replica_groups=mesh['ctx'=8,'tp'=4] {'ctx'}, use_global_device_ids=true, to_apply=%add | all-reduce | flops 512 | bytes 2048
  140.2 6.4 %copy.65 = bf16[512,4096]{0,1:T(8,128)(2,1)} copy(bf16[512,4096]{1,0:T(8,128)(2,1)} %param.17) | data formatting | bytes 8388608 | tf_op args[1]
  147.9 95.5 %all-gather.4.cloned.1.call-done = bf16[512,128,64]{1,2,0:T(8,128)(2,1)} async-done(((bf16[64,128,64]{1,2,0:T(8,128)(2,1)}), bf16[512,128,64]{1,2,0:T(8,128)(2,1)}) %all-gather.4.cloned.1.call-update) | async-done | bytes 8388624 | tf_op jit(solution)/shard_map/all_gather | solution.py:21
  245.8 49.1 %while.25 = (s32[]{:T(128)}, f32[64,128,64]{2,1,0:T(8,128)}, s32[]{:T(128)}, bf16[8,64]{1,0:T(8,128)(2,1)S(1)}, bf16[8,64,128,64]{2,3,1,0:T(8,128)(2,1)}, /*index=5*/s32[]{:T(128)}, s32[]{:T(128)}, s32[]{:T(128)}) while((s32[]{:T(128)}, f32[64,128,64]{2,1,0:T(8,128)}, s32[]{:T(128)}, bf16[8,64]{1,0:T(8,128)(2,1)S(1)}, ...), condition=%wide.region_6.7_spmd, body=%wide.region_5.6_spmd.sunk | while | flops 1572933 | bytes 9437951 | solution.py:35
  248.2 4.6 %convert_add_fusion.2 = f32[64,128,64]{2,1,0:T(8,128)} fusion(f32[64,128,64]{2,1,0:T(8,128)} %get-tuple-element.245, bf16[1,64,128,64]{3,2,1,0:T(8,128)(2,1)S(1)} %copy.90, f32[64]{0:T(128)S(1)} %exponential_bitcast_fusion.2), kind=kLoop, calls=%fused_computation.clone.1 | loop fusion | flops 1572864 | bytes 5243136 | tf_op jit(solution)/shard_map/while/body/add | solution.py:108
  255.3 4.6 %convert_add_fusion.2 = f32[64,128,64]{2,1,0:T(8,128)} fusion(f32[64,128,64]{2,1,0:T(8,128)} %get-tuple-element.245, bf16[1,64,128,64]{3,2,1,0:T(8,128)(2,1)S(1)} %copy.90, f32[64]{0:T(128)S(1)} %exponential_bitcast_fusion.2), kind=kLoop, calls=%fused_computation.clone.1 | loop fusion | flops 1572864 | bytes 5243136 | tf_op jit(solution)/shard_map/while/body/add | solution.py:108
  262.3 4.6 %convert_add_fusion.2 = f32[64,128,64]{2,1,0:T(8,128)} fusion(f32[64,128,64]{2,1,0:T(8,128)} %get-tuple-element.245, bf16[1,64,128,64]{3,2,1,0:T(8,128)(2,1)S(1)} %copy.90, f32[64]{0:T(128)S(1)} %exponential_bitcast_fusion.2), kind=kLoop, calls=%fused_computation.clone.1 | loop fusion | flops 1572864 | bytes 5243136 | tf_op jit(solution)/shard_map/while/body/add | solution.py:108
  269.3 4.6 %convert_add_fusion.2 = f32[64,128,64]{2,1,0:T(8,128)} fusion(f32[64,128,64]{2,1,0:T(8,128)} %get-tuple-element.245, bf16[1,64,128,64]{3,2,1,0:T(8,128)(2,1)S(1)} %copy.90, f32[64]{0:T(128)S(1)} %exponential_bitcast_fusion.2), kind=kLoop, calls=%fused_computation.clone.1 | loop fusion | flops 1572864 | bytes 5243136 | tf_op jit(solution)/shard_map/while/body/add | solution.py:108
  276.3 4.6 %convert_add_fusion.2 = f32[64,128,64]{2,1,0:T(8,128)} fusion(f32[64,128,64]{2,1,0:T(8,128)} %get-tuple-element.245, bf16[1,64,128,64]{3,2,1,0:T(8,128)(2,1)S(1)} %copy.90, f32[64]{0:T(128)S(1)} %exponential_bitcast_fusion.2), kind=kLoop, calls=%fused_computation.clone.1 | loop fusion | flops 1572864 | bytes 5243136 | tf_op jit(solution)/shard_map/while/body/add | solution.py:108
  283.3 4.6 %convert_add_fusion.2 = f32[64,128,64]{2,1,0:T(8,128)} fusion(f32[64,128,64]{2,1,0:T(8,128)} %get-tuple-element.245, bf16[1,64,128,64]{3,2,1,0:T(8,128)(2,1)S(1)} %copy.90, f32[64]{0:T(128)S(1)} %exponential_bitcast_fusion.2), kind=kLoop, calls=%fused_computation.clone.1 | loop fusion | flops 1572864 | bytes 5243136 | tf_op jit(solution)/shard_map/while/body/add | solution.py:108
  290.3 4.6 %convert_add_fusion.2 = f32[64,128,64]{2,1,0:T(8,128)} fusion(f32[64,128,64]{2,1,0:T(8,128)} %get-tuple-element.245, bf16[1,64,128,64]{3,2,1,0:T(8,128)(2,1)S(1)} %copy.90, f32[64]{0:T(128)S(1)} %exponential_bitcast_fusion.2), kind=kLoop, calls=%fused_computation.clone.1 | loop fusion | flops 1572864 | bytes 5243136 | tf_op jit(solution)/shard_map/while/body/add | solution.py:108
  295.0 7.8 %add_convert_fusion = bf16[4,64,128,64]{3,2,1,0:T(8,128)(2,1)S(1)} fusion(f32[4,64,128,64]{3,2,1,0:T(8,128)} %get-tuple-element.79, f32[64,128,64]{2,1,0:T(8,128)} %get-tuple-element.78, f32[4,64]{1,0:T(4,128)S(1)} %subtract_exponential_fusion), kind=kLoop, calls=%fused_computation.8 | loop fusion | flops 6291456 | bytes 14681088 | tf_op jit(solution)/shard_map/convert_element_type | solution.py:116
  302.8 5.6 %fusion.22 = f32[4,2,32,64,128]{4,3,2,1,0:T(8,128)} fusion(bf16[4,2,32,128,64]{4,3,2,1,0:T(8,128)(2,1)S(1)} %bitcast.78, bf16[4,128,2,128,1]{3,2,1,0,4:T(2,128)(2,1)S(1)} %bitcast.83), kind=kOutput, calls=%fused_computation.46 | convolution fusion | flops 536870912 | bytes 12845056 | tf_op jit(solution)/shard_map/cqgn,cgrnp->cqgrp/dot_general | solution.py:117
  311.7 12.3 %fusion.10 = f32[4,128,64,64]{1,3,2,0:T(8,128)} fusion(f32[4,128,64,64]{1,3,2,0:T(8,128)} %bitcast.80, f32[64]{0:T(128)S(1)} %copy-done.8, f32[4,128,64]{1,2,0:T(8,128)} %copy.54, f32[4,64,128,128]{3,2,1,0:T(8,128)S(1)} %bitcast.79, f32[4,64,128]{2,1,0:T(8,128)} %copy.52, f32[4,64,128]{2,1,0:T(8,128)} %copy.49, pred[128,128]{1,0:T(8,128)(4,1)S(1)} %iota_compare_fusion, ...), kind=kOutput, calls=%fused_computation.24 | convolution fusion | flops 568328192 | bytes 38158592 | tf_op jit(solution)/shard_map/chqs,cshp->cqhp/dot_general | solution.py:90
  323.9 14.7 %copy.64 = f32[4,128,64,64]{1,0,3,2:T(4,128)} copy(f32[4,128,64,64]{1,3,2,0:T(8,128)} %fusion.10) | data formatting | bytes 16777216 | tf_op jit(solution)/shard_map/add | solution.py:121
  338.7 5.9 %bitcast_reduce_fusion = f32[512,2]{0,1:T(2,128)S(1)} fusion(bf16[512,4096]{0,1:T(8,128)(2,1)S(1)} %copy-done.1, f32[512,8,4,128]{3,2,1,0:T(4,128)} %bitcast.75), kind=kLoop, calls=%fused_computation.22 | loop fusion | flops 16776192 | bytes 12587008 | tf_op jit(solution)/shard_map/reduce_sum | solution.py:124
  347.5 23.5 %convolution_convert_fusion = bf16[512,4096]{1,0:T(8,128)(2,1)} fusion(bf16[512,4096]{0,1:T(8,128)(2,1)S(1)} %fusion.9, bf16[4096,4096]{1,0:T(8,128)(2,1)} %param.27), kind=kOutput, calls=%fused_computation.34 | convolution fusion | flops 17181966336 | bytes 41943040 | tf_op jit(solution)/shard_map/dot_general | solution.py:129
  371.0 45.7 %reduce-scatter.2.cloned.1.call-done = bf16[128,4096]{1,0:T(8,128)(2,1)} async-done(((bf16[512,4096]{1,0:T(8,128)(2,1)}), bf16[128,4096]{1,0:T(8,128)(2,1)}) %reduce-scatter.2.cloned.1.call-update) | async-done | bytes 1048592 | tf_op jit(solution)/shard_map/reduce_scatter | solution.py:128
  (91 shorter events, 47.7 us)
Async XLA Ops:
  6.5 15.8 %copy-start.4 = (bf16[512,2,256]{2,1,0:T(2,128)(2,1)S(1)}, bf16[512,2,256]{2,1,0:T(2,128)(2,1)}, u32[]{:S(2)}) copy-start(bf16[512,2,256]{2,1,0:T(2,128)(2,1)} %param.18) | copy-start | bytes 1572868
  6.5 16.2 %copy-start.7 = (f32[2,256]{1,0:T(2,128)S(1)}, f32[2,256]{1,0:T(2,128)}, u32[]{:S(2)}) copy-start(f32[2,256]{1,0:T(2,128)} %param.25) | copy-start | bytes 6148
  6.5 236.8 %all-gather.4.cloned.1.call-start = ((), (), s32[]{:S(2)}) async-start(), calls=%async_computation.2 | async-start | bytes 9437184 | tf_op jit(solution)/shard_map/all_gather | solution.py:21
  7.3 15.0 %collective-permute-start.1 = (bf16[3,2,256]{2,1,0:T(2,128)(2,1)S(1)}, bf16[3,2,256]{2,1,0:T(2,128)(2,1)S(1)}, u32[]{:S(2)}, u32[]{:S(2)}) collective-permute-start(bf16[3,2,256]{2,1,0:T(2,128)(2,1)S(1)} %slice.67), channel_id=1, source_target_pairs={{0,4},{4,8},{8,12},{12,16},{16,20},{20,24},{24,28},{1,5},{5,9},{9,... | collective-permute-start | bytes 9224 | tf_op jit(solution)/shard_map/ppermute | solution.py:15
  9.5 18.1 %collective-permute-start = (bf16[3,4096]{1,0:T(4,128)(2,1)S(1)}, bf16[3,4096]{1,0:T(4,128)(2,1)S(1)}, u32[]{:S(2)}, u32[]{:S(2)}) collective-permute-start(bf16[3,4096]{1,0:T(4,128)(2,1)S(1)} %slice.59), channel_id=1, source_target_pairs={{0,4},{4,8},{8,12},{12,16},{16,20},{20,24},{24,28},{1,5},{5,9},{9,... | collective-permute-start | bytes 73736 | tf_op jit(solution)/shard_map/ppermute | solution.py:15
  15.0 13.1 %copy-start.5 = (f32[4096]{0:T(1024)S(1)}, f32[4096]{0:T(1024)}, u32[]{:S(2)}) copy-start(f32[4096]{0:T(1024)} %param.23) | copy-start | bytes 49156
  50.9 7.8 %copy-start.2 = (bf16[4,128,64,64]{1,0,3,2:T(4,128)(2,1)S(1)}, bf16[4,128,64,64]{1,0,3,2:T(4,128)(2,1)}, u32[]{:S(2)}) copy-start(bf16[4,128,64,64]{1,0,3,2:T(4,128)(2,1)} %reshape.103) | copy-start | bytes 12582916
  74.6 42.6 %copy-start.9 = (u32[32]{0:T(128)S(1)}, u32[32]{0:T(128)}, u32[]{:S(2)}) copy-start(u32[32]{0:T(128)} %constant.63) | copy-start | bytes 388
  116.9 299.7 %reduce-scatter.2.cloned.1.call-start = ((), (), s32[]{:S(2)}) async-start(), calls=%async_computation.1 | async-start | bytes 5242880 | tf_op jit(solution)/shard_map/reduce_scatter | solution.py:128
  308.3 3.3 copy-start.3
  308.3 3.3 copy-start.8
  323.9 14.8 %copy-start.1 = (bf16[512,4096]{0,1:T(8,128)(2,1)S(1)}, bf16[512,4096]{0,1:T(8,128)(2,1)}, u32[]{:S(2)}) copy-start(bf16[512,4096]{0,1:T(8,128)(2,1)} %copy.65) | copy-start | bytes 12582916
  338.7 5.9 %copy-start = (f32[4,128,64,64]{1,0,3,2:T(4,128)S(1)}, f32[4,128,64,64]{1,0,3,2:T(4,128)}, u32[]{:S(2)}) copy-start(f32[4,128,64,64]{1,0,3,2:T(4,128)} %copy.64) | copy-start | bytes 25165828
  338.7 5.9 %copy-start.6 = (f32[4096]{0:T(1024)S(1)}, f32[4096]{0:T(1024)}, u32[]{:S(2)}) copy-start(f32[4096]{0:T(1024)} %param.26) | copy-start | bytes 49156
Sparse Core Ops, SparseCore 0:
  117.1 126.2 all-gather.3
  371.1 45.5 reduce-scatter.1
where the time goes:
time: 427 us; the launch traced here: 424 us
  waiting for transfers between devices  141 us (33%)
  other arithmetic  108 us (25%)
  local copies, waits for them, and re-layouts  79.4 us (19%)
  matrix products  58.3 us (14%)
  blocking collectives  19 us (4%)
  between operations  14.4 us (3%)
    all_gather x1, waiting for transfers between devices, carried_in(): lax.all_gather(a.astype(kind), axis)  95.5 us
    reduce_scatter x1, waiting for transfers between devices, local(): lax.psum_scatter(jnp.dot(normed, out_weight, preferred_element_type=jnp.f...  45.7 us
    add x7, other arithmetic, combine(): jnp.exp(latter[0])[:, None, None] * earlier[1] + latter[1]  32.3 us
    dot_general x1, matrix products, local(): jnp.dot(normed, out_weight, preferred_element_type=jnp.float32)  23.5 us
    add x4, other arithmetic, advance(): jnp.exp(block_total)[:, None, None] * carry_state + new_part  22.3 us
    unnamed x1, blocking collectives  19 us
    convert_element_type x2, other arithmetic, causal_conv(): return jax.nn.silu(accum).astype(jnp.bfloat16)  18.4 us
    dynamic_slice x14, local copies, waits for them, and re-layouts, one(): lax.dynamic_index_in_dim(a, step, 0, False).astype(own.dtype)  16.6 us
  transfers between devices with their start and end apart: 4, of which 2 were waited for; matrix products, arithmetic and copies ran while one was open for 7% of the time, Pallas kernels for 0%

commit v1 on v0

v1 whole, which is shorter than its diff:
```python
import functools

import jax
import jax.numpy as jnp
from jax import lax
from jax.experimental import pallas as pl
from jax.experimental.pallas import tpu as pltpu
from jax.sharding import PartitionSpec as P

HEAD_DIM = 64
STATE = 128
CONV = 4
BLOCK = 128
WIDE = 512
LEAD = 8
HEADS = 64
F32 = jnp.float32
BF16 = jnp.bfloat16
MESH = pl.DeviceIdType.MESH


def silu(v):
    return v / (1.0 + jnp.exp(-v))


def dot(a, b):
    return jnp.dot(a, b, preferred_element_type=F32)


def two_parts(v):
    high = v.astype(BF16)
    low = (v - high.astype(F32)).astype(BF16)
    return jnp.concatenate([high, low], axis=1)


def spread_matrix(chunk, heads):
    rows = lax.broadcasted_iota(jnp.int32, (2 * heads, WIDE), 0)
    cols = lax.broadcasted_iota(jnp.int32, (2 * heads, WIDE), 1)
    rows = jnp.where(rows >= heads, rows - heads, rows)
    return jnp.where(rows == chunk * (WIDE // HEAD_DIM) + cols // HEAD_DIM, 1.0, 0.0).astype(BF16)


def conv_rows(padded, base, count, weight, bias):
    window = padded[pl.ds(base, count + LEAD), :]
    total = bias
    for tap in range(CONV):
        start = LEAD - CONV + 1 + tap
        total = total + weight[tap : tap + 1] * window[start : start + count]
    return silu(total)


def state_kernel(
    x_ref, lead_ref, cw_ref, cb_ref, maps_ref, mlead_ref, mw_ref, mb_ref, step_ref, rate_ref,
    xc_ref, mc_ref, bt_ref, rs_ref, s_ref, enter_ref, padded, mpadded, load, tot,
):
    chunk = pl.program_id(0)
    length = x_ref.shape[0]
    heads = step_ref.shape[1]
    blocks = length // BLOCK
    groups = bt_ref.shape[0]
    per_group = pl.num_programs(0) // groups
    half = 64

    @pl.when(chunk == 0)
    def _():
        mpadded[0:LEAD] = mlead_ref[...].astype(F32)
        mpadded[LEAD:] = maps_ref[...].astype(F32)
        for r in range(length // half):
            mapped = conv_rows(mpadded, r * half, half, mw_ref[...], mb_ref[...])
            mc_ref[r * half : (r + 1) * half] = mapped.astype(BF16)
        tri = (
            lax.broadcasted_iota(jnp.int32, (BLOCK, BLOCK), 0)
            >= lax.broadcasted_iota(jnp.int32, (BLOCK, BLOCK), 1)
        ).astype(F32)
        for b in range(blocks):
            rows = slice(b * BLOCK, (b + 1) * BLOCK)
            for g in range(groups):
                own = mc_ref[rows, g * STATE : (g + 1) * STATE].astype(F32)
                bt_ref[g, :, rows] = own.T.astype(BF16)
            step = step_ref[rows]
            running = jnp.dot(
                tri, -rate_ref[...] * step,
                precision=lax.Precision.HIGHEST, preferred_element_type=F32,
            )
            rs_ref[rows] = jnp.concatenate([running, step], axis=1)
            last = running[BLOCK - 1 : BLOCK]
            load[rows] = two_parts(jnp.exp(last - running) * step)
            tot[b] = jnp.broadcast_to(two_parts(jnp.exp(last)).astype(F32), (8, 2 * heads))

    spread = spread_matrix(chunk, heads)
    padded[0:LEAD] = lead_ref[...].astype(F32)

    def widen(r, _):
        at = pl.multiple_of(r * half, half)
        padded[pl.ds(at + LEAD, half), :] = x_ref[pl.ds(at, half), :].astype(F32)
        return 0

    lax.fori_loop(0, length // half, widen, 0)
    weight, bias = cw_ref[...], cb_ref[...]

    def conv(r, _):
        at = pl.multiple_of(r * half, half)
        xc_ref[pl.ds(at, half), :] = conv_rows(padded, at, half, weight, bias).astype(BF16)
        return 0

    lax.fori_loop(0, length // half, conv, 0)
    group = chunk // per_group
    state = jnp.zeros((STATE, WIDE), F32)
    for b in range(blocks):
        rows = slice(b * BLOCK, (b + 1) * BLOCK)
        if b > 0:
            enter_ref[b - 1, 0] = state.astype(BF16)
        scaled = (xc_ref[rows].astype(F32) * dot(load[rows], spread)).astype(BF16)
        fresh = dot(bt_ref[group, :, rows], scaled)
        if b > 0:
            keep = dot(tot[b].astype(BF16), spread)[0:1]
            state = keep * state + fresh
        else:
            state = fresh
    s_ref[0] = state.astype(BF16)


def within_kernel(
    pairs, xc_ref, mc_ref, bt_ref, rs_ref, skip_ref, s_ref, y_ref, inc_ref,
    rolled, flipped, scores, mine, theirs, got, chain_in, chain_out, back_out, back_in,
    log_send, log_recv, x_send, x_recv, c_send, c_recv, b_send, b_recv,
):
    i = pl.program_id(0)
    steps = pl.num_programs(0)
    length = rs_ref.shape[0]
    heads = rs_ref.shape[1] // 2
    blocks = length // BLOCK
    groups = bt_ref.shape[0]
    chunks = s_ref.shape[0]
    per_half = chunks // 2
    per_group = chunks // groups
    place = lax.axis_index("ctx")
    pair, side = place // 2, place % 2
    peer = {"ctx": pair * 2 + 1 - side}
    ahead = {"ctx": place + 2}
    behind = {"ctx": place - 2}

    def log_copy():
        return pltpu.make_async_remote_copy(
            mine, theirs, log_send, log_recv, device_id=peer, device_id_type=MESH
        )

    def x_copy(c):
        return pltpu.make_async_remote_copy(
            s_ref.at[(1 - side) * per_half + c], got.at[c], x_send.at[c], x_recv.at[c],
            device_id=peer, device_id_type=MESH,
        )

    def c_copy(c):
        return pltpu.make_async_remote_copy(
            chain_out.at[c], chain_in.at[c], c_send.at[c], c_recv.at[c],
            device_id=ahead, device_id_type=MESH,
        )

    def b_copy(c):
        return pltpu.make_async_remote_copy(
            back_out.at[c], back_in.at[c], b_send.at[c], b_recv.at[c],
            device_id=peer, device_id_type=MESH,
        )

    @pl.when(i == 0)
    def _():
        barrier = pltpu.get_barrier_semaphore()
        pl.semaphore_signal(barrier, inc=1, device_id=peer, device_id_type=MESH)

        @pl.when(pair > 0)
        def _():
            pl.semaphore_signal(barrier, inc=1, device_id=behind, device_id_type=MESH)

        @pl.when(pair < pairs - 1)
        def _():
            pl.semaphore_signal(barrier, inc=1, device_id=ahead, device_id_type=MESH)

        total = jnp.zeros((1, heads), F32)
        for b in range(blocks):
            total = total + rs_ref[(b + 1) * BLOCK - 1 : (b + 1) * BLOCK, 0:heads]
        keep = jnp.exp(total)
        mine[...] = jnp.broadcast_to(jnp.concatenate([keep, keep], axis=1), (8, 2 * heads))
        near = jnp.where(pair > 0, 1, 0) + jnp.where(pair < pairs - 1, 1, 0) + 1
        pl.semaphore_wait(barrier, near)
        log_copy().start()
        for c in range(per_half):
            x_copy(c).start()

    c = i - 1 - 2 * pair

    @pl.when(i == 1)
    def _():
        log_copy().wait_recv()

    @pl.when((c >= 0) & (c < per_half))
    def _():
        x_copy(c).wait_recv()

        @pl.when(pair > 0)
        def _():
            c_copy(c).wait_recv()

        spread = spread_matrix(side * per_half + c, heads)
        keep_mine = dot(two_parts(mine[:, 0:heads]), spread)[0:1]
        keep_theirs = dot(two_parts(theirs[:, 0:heads]), spread)[0:1]
        own = s_ref[side * per_half + c].astype(F32)
        other = got[c].astype(F32)
        early = side == 0
        first = jnp.where(early, own, other)
        second = jnp.where(early, other, own)
        keep_first = jnp.where(early, keep_mine, keep_theirs)
        keep_second = jnp.where(early, keep_theirs, keep_mine)
        before = jnp.where(pair > 0, chain_in[c].astype(F32), 0.0)
        middle = keep_first * before + first
        after = keep_second * middle + second
        back_out[c] = jnp.where(early, middle, before).astype(BF16)
        b_copy(c).start()

        @pl.when(pair < pairs - 1)
        def _():
            chain_out[c] = after.astype(BF16)
            c_copy(c).start()

        inc_ref[side * per_half + c] = jnp.where(early, before, middle).astype(BF16)

    @pl.when(i < chunks)
    def _():
        wide = pltpu.roll(rs_ref[...], (2 * heads - i * (WIDE // HEAD_DIM)) % (2 * heads), 1)
        rolled[...] = wide
        flipped[...] = wide.T
        group = i // per_group

        def block(b, _):
            at = pl.multiple_of(b * BLOCK, BLOCK)
            rows = pl.ds(at, BLOCK)
            out_map = mc_ref[rows, pl.ds(pl.multiple_of((groups + group) * STATE, STATE), STATE)]
            score = dot(out_map, bt_ref[group, :, rows])
            causal = (
                lax.broadcasted_iota(jnp.int32, (BLOCK, BLOCK), 0)
                >= lax.broadcasted_iota(jnp.int32, (BLOCK, BLOCK), 1)
            )
            lower = lax.broadcasted_iota(jnp.int32, (BLOCK, 2 * HEAD_DIM), 1) < HEAD_DIM
            columns = rolled[rows, :]
            for p in range(WIDE // (2 * HEAD_DIM)):
                parts = []
                for h in (2 * p, 2 * p + 1):
                    gap = columns[:, h : h + 1] - flipped[h : h + 1, rows]
                    decay = jnp.exp(jnp.where(causal, gap, -1e30))
                    parts.append((score * decay * flipped[heads + h : heads + h + 1, rows]).astype(BF16))
                lanes = slice(p * 2 * HEAD_DIM, (p + 1) * 2 * HEAD_DIM)
                x = xc_ref[rows, lanes]
                zero = jnp.zeros_like(x)
                both = jnp.concatenate([jnp.where(lower, x, zero), jnp.where(lower, zero, x)], axis=0)
                y = dot(jnp.concatenate(parts, axis=1), both)
                y_ref[rows, lanes] = (y + skip_ref[:, lanes] * x.astype(F32)).astype(BF16)
            return 0

        lax.fori_loop(0, blocks, block, 0)

    @pl.when(i == steps - 1)
    def _():
        log_copy().wait_send()

        def finish(c, _):
            x_copy(c).wait_send()
            b_copy(c).wait_send()
            b_copy(c).wait_recv()
            inc_ref[(1 - side) * per_half + c] = back_in[c]

            @pl.when(pair < pairs - 1)
            def _():
                c_copy(c).wait_send()

            return 0

        lax.fori_loop(0, per_half, finish, 0)


def norm_kernel(
    y_ref, gate_ref, mc_ref, rs_ref, enter_ref, inc_ref, gain_ref, out_ref,
    gated, square, reach, prior,
):
    g, j = pl.program_id(0), pl.program_id(1)
    per_group = pl.num_programs(1)
    groups = pl.num_programs(0)
    length = rs_ref.shape[0]
    heads = rs_ref.shape[1] // 2
    blocks = length // BLOCK

    @pl.when((g == 0) & (j == 0))
    def _():
        total = jnp.zeros((1, heads), F32)
        for b in range(blocks):
            rows = slice(b * BLOCK, (b + 1) * BLOCK)
            running = rs_ref[rows, 0:heads]
            reach[rows] = two_parts(jnp.exp(running))
            prior[b] = jnp.broadcast_to(two_parts(jnp.exp(total)).astype(F32), (8, 2 * heads))
            total = total + running[BLOCK - 1 : BLOCK]

    spread = spread_matrix(g * per_group + j, heads)
    out_maps = mc_ref[...]
    for b in range(blocks):
        rows = slice(b * BLOCK, (b + 1) * BLOCK)
        incoming = inc_ref[0].astype(F32)
        if b > 0:
            keep = dot(prior[b].astype(BF16), spread)[0:1]
            incoming = keep * incoming + enter_ref[b - 1, 0].astype(F32)
        before = dot(out_maps[rows], incoming.astype(BF16))
        value = y_ref[rows].astype(F32) + dot(reach[rows], spread) * before
        value = value * silu(gate_ref[rows].astype(F32))
        gated[j, rows] = value
        part = jnp.sum(value * value, axis=1, keepdims=True)
        part = jnp.broadcast_to(part, (BLOCK, 128))

        @pl.when(j == 0)
        def _():
            square[rows] = part

        @pl.when(j > 0)
        def _():
            square[rows] = square[rows] + part

    @pl.when(j == per_group - 1)
    def _():
        for b in range(blocks):
            rows = slice(b * BLOCK, (b + 1) * BLOCK)
            mean = square[rows][:, 0:1] * (1.0 / (per_group * WIDE))
            inverse = lax.rsqrt(mean + 1e-05)
            for k in range(out_ref.shape[1] // WIDE):
                lanes = slice(k * WIDE, (k + 1) * WIDE)
                out_ref[rows, lanes] = (gated[k, rows] * inverse * gain_ref[:, lanes]).astype(BF16)


def project_kernel(
    tiles, fars, a_ref, w_ref, o_ref, part, send, recv, hop_keep, hop_send, hop_recv,
    s_send, s_recv, h_send, h_recv,
):
    i = pl.program_id(0)
    place = lax.axis_index("tp")
    far, core = place // 2, place % 2
    peer = {"tp": far * 2 + 1 - core}
    share = o_ref.shape[0]

    def across(d):
        return {"tp": (far + d) % fars * 2 + core}

    def near_copy(t):
        return pltpu.make_async_remote_copy(
            send.at[t], recv.at[t], s_send.at[t], s_recv.at[t],
            device_id=peer, device_id_type=MESH,
        )

    def far_copy(t, d):
        at = t * (fars - 1) + d - 1
        return pltpu.make_async_remote_copy(
            hop_send.at[at], hop_recv.at[at], h_send.at[at], h_recv.at[at],
            device_id=across(d), device_id_type=MESH,
        )

    @pl.when(i == 0)
    def _():
        barrier = pltpu.get_barrier_semaphore()
        pl.semaphore_signal(barrier, inc=1, device_id=peer, device_id_type=MESH)
        for d in range(1, fars):
            pl.semaphore_signal(barrier, inc=1, device_id=across(d), device_id_type=MESH)
        pl.semaphore_wait(barrier, fars)

    @pl.when(i < tiles)
    def _():
        part[i % 2] = dot(a_ref[...], w_ref[...])
        for q in range(fars):
            theirs = pl.multiple_of((q * 2 + 1 - core) * share, share)
            send[i, q] = part[i % 2, pl.ds(theirs, share), :].astype(BF16)
        near_copy(i).start()

    @pl.when((i >= 1) & (i < tiles + 1))
    def _():
        t = i - 1
        near_copy(t).wait_recv()
        for d in range(1, fars):
            q = (far + d) % fars
            own = pl.multiple_of((q * 2 + core) * share, share)
            total = part[t % 2, pl.ds(own, share), :] + recv[t, q].astype(F32)
            hop_send[t * (fars - 1) + d - 1] = total.astype(BF16)
            far_copy(t, d).start()
        own = pl.multiple_of((far * 2 + core) * share, share)
        hop_keep[t] = part[t % 2, pl.ds(own, share), :] + recv[t, far].astype(F32)

    @pl.when(i >= 3)
    def _():
        t = i - 3
        total = hop_keep[t]
        for d in range(1, fars):
            far_copy(t, d).wait_recv()
            total = total + hop_recv[t * (fars - 1) + d - 1].astype(F32)
        o_ref[...] = total.astype(BF16)
        near_copy(t).wait_send()
        for d in range(1, fars):
            far_copy(t, d).wait_send()


def whole(shape):
    return pl.BlockSpec(shape, lambda *_: (0,) * len(shape))


def local(
    ctx_size, tp_size, ssm_input, gate_input, state_maps, step_size, decay_rate, skip_gain, conv_weight,
    conv_bias, map_conv, map_bias, norm_gain, out_weight,
):
    length, width = ssm_input.shape
    step_size = jnp.pad(step_size, ((0, 0), (0, HEADS - step_size.shape[1])))
    decay_rate = jnp.pad(decay_rate, (0, HEADS - decay_rate.shape[0]))
    heads = HEADS
    groups = state_maps.shape[2] // STATE
    blocks = length // BLOCK
    chunks = width // WIDE
    per_group = chunks // groups
    maps_width = 2 * groups * STATE
    maps = state_maps.reshape(length, maps_width)
    tail = jnp.concatenate([ssm_input[length - LEAD :], maps[length - LEAD :]], axis=1)
    lead = lax.ppermute(tail, "ctx", [(k, k + 1) for k in range(ctx_size - 1)])
    limit = pltpu.CompilerParams(vmem_limit_bytes=56 * 1024 * 1024)
    shape = jax.ShapeDtypeStruct
    cols = lambda j: (0, j)
    xc, mc, bt, rs, s, enter = pl.pallas_call(
        state_kernel,
        grid=(chunks,),
        in_specs=[
            pl.BlockSpec((length, WIDE), cols),
            pl.BlockSpec((LEAD, WIDE), cols),
            pl.BlockSpec((CONV, WIDE), cols),
            pl.BlockSpec((1, WIDE), cols),
            whole((length, maps_width)),
            pl.BlockSpec((LEAD, maps_width), lambda j: (0, width // maps_width)),
            whole((CONV, maps_width)),
            whole((1, maps_width)),
            whole((length, heads)),
            whole((1, heads)),
        ],
        out_specs=[
            pl.BlockSpec((length, WIDE), cols),
            whole((length, maps_width)),
            whole((groups, STATE, length)),
            whole((length, 2 * heads)),
            pl.BlockSpec((1, STATE, WIDE), lambda j: (j, 0, 0)),
            pl.BlockSpec((blocks - 1, 1, STATE, WIDE), lambda j: (0, j, 0, 0)),
        ],
        out_shape=[
            shape((length, width), BF16),
            shape((length, maps_width), BF16),
            shape((groups, STATE, length), BF16),
            shape((length, 2 * heads), F32),
            shape((chunks, STATE, WIDE), BF16),
            shape((blocks - 1, chunks, STATE, WIDE), BF16),
        ],
        scratch_shapes=[
            pltpu.VMEM((length + LEAD, WIDE), F32),
            pltpu.VMEM((length + LEAD, maps_width), F32),
            pltpu.VMEM((length, 2 * heads), BF16),
            pltpu.VMEM((blocks, 8, 2 * heads), F32),
        ],
        compiler_params=limit,
        name="state",
    )(
        ssm_input, lead, conv_weight, conv_bias[None], maps, lead,
        map_conv.reshape(CONV, maps_width), map_bias.reshape(1, maps_width), step_size,
        decay_rate[None],
    )
    pairs = ctx_size // 2
    per_half = chunks // 2
    steps = max(chunks, per_half + 1 + 2 * (pairs - 1)) + 1
    held = lambda i: (0, jnp.minimum(i, chunks - 1))
    slab = (per_half, STATE, WIDE)
    dma = pltpu.SemaphoreType.DMA
    y, incoming = pl.pallas_call(
        functools.partial(within_kernel, pairs),
        grid=(steps,),
        in_specs=[
            pl.BlockSpec((length, WIDE), held),
            whole((length, maps_width)),
            whole((groups, STATE, length)),
            whole((length, 2 * heads)),
            pl.BlockSpec((1, WIDE), held),
            whole((chunks, STATE, WIDE)),
        ],
        out_specs=[pl.BlockSpec((length, WIDE), held), whole((chunks, STATE, WIDE))],
        out_shape=[shape((length, width), BF16), shape((chunks, STATE, WIDE), BF16)],
        scratch_shapes=[
            pltpu.VMEM((length, 2 * heads), F32),
            pltpu.VMEM((2 * heads, length), F32),
            pltpu.VMEM((8, BLOCK), F32),
            pltpu.VMEM((8, 2 * heads), F32),
            pltpu.VMEM((8, 2 * heads), F32),
            pltpu.VMEM(slab, BF16),
            pltpu.VMEM(slab, BF16),
            pltpu.VMEM(slab, BF16),
            pltpu.VMEM(slab, BF16),
            pltpu.VMEM(slab, BF16),
            dma, dma,
        ] + [dma((per_half,))] * 6,
        compiler_params=pltpu.CompilerParams(
            collective_id=0, has_side_effects=True, vmem_limit_bytes=56 * 1024 * 1024
        ),
        name="within",
    )(xc, mc, bt, rs, jnp.repeat(skip_gain, HEAD_DIM)[None], s)
    at = lambda g, j: (0, g * per_group + j)
    normed = pl.pallas_call(
        norm_kernel,
        grid=(groups, per_group),
        in_specs=[
            pl.BlockSpec((length, WIDE), at),
            pl.BlockSpec((length, WIDE), at),
            pl.BlockSpec((length, STATE), lambda g, j: (0, groups + g)),
            whole((length, 2 * heads)),
            pl.BlockSpec((blocks - 1, 1, STATE, WIDE), lambda g, j: (0, g * per_group + j, 0, 0)),
            pl.BlockSpec((1, STATE, WIDE), lambda g, j: (g * per_group + j, 0, 0)),
            pl.BlockSpec((1, width // groups), lambda g, j: (0, g)),
        ],
        out_specs=pl.BlockSpec((length, width // groups), lambda g, j: (0, g)),
        out_shape=shape((length, width), BF16),
        scratch_shapes=[
            pltpu.VMEM((per_group, length, WIDE), F32),
            pltpu.VMEM((length, 128), F32),
            pltpu.VMEM((length, 2 * heads), BF16),
            pltpu.VMEM((blocks, 8, 2 * heads), F32),
        ],
        compiler_params=limit,
        name="norm",
    )(y, gate_input, mc, rs, enter, incoming, norm_gain[None])
    d_out = out_weight.shape[1]
    tiles = d_out // WIDE
    share = length // tp_size
    fars = tp_size // 2
    hops = tiles * (fars - 1)
    return pl.pallas_call(
        functools.partial(project_kernel, tiles, fars),
        grid=(tiles + 3,),
        in_specs=[
            whole((length, width)),
            pl.BlockSpec((width, WIDE), lambda i: (0, jnp.minimum(i, tiles - 1))),
        ],
        out_specs=pl.BlockSpec((share, WIDE), lambda i: (0, jnp.maximum(i - 3, 0))),
        out_shape=shape((share, d_out), BF16),
        scratch_shapes=[
            pltpu.VMEM((2, length, WIDE), F32),
            pltpu.VMEM((tiles, fars, share, WIDE), BF16),
            pltpu.VMEM((tiles, fars, share, WIDE), BF16),
            pltpu.VMEM((tiles, share, WIDE), F32),
            pltpu.VMEM((hops, share, WIDE), BF16),
            pltpu.VMEM((hops, share, WIDE), BF16),
        ] + [dma((tiles,))] * 2 + [dma((hops,))] * 2,
        compiler_params=pltpu.CompilerParams(
            collective_id=1, has_side_effects=True, vmem_limit_bytes=56 * 1024 * 1024
        ),
        name="project",
    )(normed, out_weight)


def solution(mesh):
    in_specs = (
        P("ctx", "tp"), P("ctx", "tp"), P("ctx", None, "tp"), P("ctx", "tp"), P("tp"), P("tp"),
        P(None, "tp"), P("tp"), P(None, None, "tp"), P(None, "tp"), P("tp"), P("tp", None),
    )
    return jax.shard_map(
        functools.partial(local, mesh.shape["ctx"], mesh.shape["tp"]), mesh=mesh, in_specs=in_specs,
        out_specs=P(("ctx", "tp"), None), check_vma=False,
    )
```

time: 427 us -> 126 us (0.30)
  waiting for transfers between devices: 141 us -> 0.01 us
  Pallas kernels: 0 us -> 113 us
  other arithmetic: 108 us -> 0.01 us
  local copies, waits for them, and re-layouts: 79.4 us -> 12 us
  matrix products: 58.3 us -> 0 us
  blocking collectives: 19 us -> 0 us
  between operations: 14.4 us -> 0.04 us
    pallas_call x0 -> x4, Pallas kernels: none -> 113 us  [the longest x1 36.4 us: local(): pl.pallas_call(functools.partial(within_kernel, pairs), grid=(steps,), in...]
    all_gather x1 -> x0, waiting for transfers between devices: 95.5 us -> none  [carried_in(): lax.all_gather(a.astype(kind), axis)]
    dot_general x5 -> x0, matrix products: 58.3 us -> none  [the longest x1 23.5 us: local(): jnp.dot(normed, out_weight, preferred_element_type=jnp.float32)]
    add x11 -> x0, other arithmetic: 54.7 us -> none  [the longest x7 32.3 us: combine(): jnp.exp(latter[0])[:, None, None] * earlier[1] + latter[1]]
    reduce_scatter x1 -> x0, waiting for transfers between devices: 45.7 us -> none  [local(): lax.psum_scatter(jnp.dot(normed, out_weight, preferred_element_type=jnp.f...]
    convert_element_type x4 -> x0, other arithmetic: 29.1 us -> none  [the longest x2 18.4 us: causal_conv(): return jax.nn.silu(accum).astype(jnp.bfloat16)]
    unnamed x1 -> x0, blocking collectives: 19 us -> none
    dynamic_slice x14 -> x0, local copies, waits for them, and re-layouts: 16.6 us -> none  [one(): lax.dynamic_index_in_dim(a, step, 0, False).astype(own.dtype)]
  transfers between devices with their start and end apart: 4 -> 1, of which waited for: 2 -> 0; matrix products, arithmetic and copies ran while one was open for 7% -> 6% of each run, Pallas kernels for 0% -> 0%
where the time goes in v1:
time: 126 us
  Pallas kernels  113 us (90%)
  local copies, waits for them, and re-layouts  12 us (10%)
  starting transfers between devices  1.29 us (1%)
    pallas_call x1, Pallas kernels, local(): pl.pallas_call(functools.partial(within_kernel, pairs), grid=(steps,), in...  36.4 us
    pallas_call x1, Pallas kernels, local(): pl.pallas_call(functools.partial(project_kernel, tiles, fars), grid=(tile...  34.6 us
    pallas_call x1, Pallas kernels, local(): pl.pallas_call(state_kernel, grid=(chunks,), in_specs=[pl.BlockSpec((leng...  22.8 us
    pallas_call x1, Pallas kernels, local(): pl.pallas_call(norm_kernel, grid=(groups, per_group), in_specs=[pl.BlockS...  18.8 us
    unnamed x9, local copies, waits for them, and re-layouts  9.78 us
  transfers between devices with their start and end apart: 1, of which 0 were waited for; matrix products, arithmetic and copies ran while one was open for 6% of the time, Pallas kernels for 0%

profile of v1, /device:TPU:26, one launch (start us, length us, event | category | flops | bytes accessed | tf_op | source)
XLA Modules:
  0.0 126.0 jit_solution(13861291481699877314)
XLA Ops:
  0.0 0.7 slice_bitcast_fusion
  0.7 0.8 slice.9
  1.6 1.3 %collective-permute-start = (bf16[8,4608]{1,0:T(8,128)(2,1)S(1)}, bf16[8,4608]{1,0:T(8,128)(2,1)S(1)}, u32[]{:S(2)}, u32[]{:S(2)}) collective-permute-start(bf16[8,4608]{1,0:T(8,128)(2,1)S(1)} %pad_maximum_fusion), channel_id=1, source_target_pairs={{0,4},{4,8},{8,12},{12,16},{16,20},{20,24},{24,28},{1,5},{5,9},{9,... | collective-permute-start | bytes 221192 | tf_op jit(solution)/shard_map/ppermute | solution.py:422
  2.9 1.2 copy.17
  4.1 1.3 %copy.16 = f32[1,4,2,256]{3,1,2,0:T(4,128)} copy(f32[1,4,2,256]{3,2,1,0:T(2,128)} %bitcast.20) | data formatting | bytes 16384
  5.4 0.7 broadcast_in_dim.14
  6.1 0.7 broadcast_in_dim_reshape.3.skip_ref
  6.8 1.7 %copy.13.step_ref = f32[512,64]{1,0:T(8,128)} copy(f32[512,64]{0,1:T(8,128)} %param.15) | data formatting | bytes 262144 | tf_op args[3]
  8.5 1.9 %copy.15 = bf16[64,8,2,256]{3,1,2,0:T(8,128)(2,1)} copy(bf16[64,8,2,256]{3,2,1,0:T(2,128)(2,1)} %bitcast.14) | data formatting | bytes 1048576
  10.4 0.0 collective-permute-done.lead_ref.mlead_ref
  10.4 0.0 copy-start
  10.4 0.6 copy-done
  11.1 22.8 %state.1 = (bf16[512,4096]{1,0:T(8,128)(2,1)}, bf16[512,512]{1,0:T(8,128)(2,1)}, bf16[2,128,512]{2,1,0:T(8,128)(2,1)}, f32[512,128]{1,0:T(8,128)}, bf16[8,128,51...) custom-call(bf16[512,4096]{1,0:T(8,128)(2,1)} %x_ref.1, bf16[8,4608]{1,0:T(8,128)(2,1)} %copy-done, f32[4,4096]{1,0:T(4,128)} %cw_ref.1, ...), custom_call_target="tpu_custom_call" | custom-call | tf_op jit(solution)/shard_map/state/pallas_call | solution.py:426
  33.9 36.4 %within.1 = (bf16[512,4096]{1,0:T(8,128)(2,1)}, bf16[8,128,512]{2,1,0:T(8,128)(2,1)}) custom-call(bf16[512,4096]{1,0:T(8,128)(2,1)} %get-tuple-element.13.xc_ref, bf16[512,512]{1,0:T(8,128)(2,1)} %get-tuple-element.14.mc_ref, bf16[2,128,512]{2,1,0:T(8,128)(2,1)} %get-tuple-element.15.bt_ref, f32[512,128]{1,0:T(8,128)} %get-tuple-element.16.rs_ref, ...), custom_call_target="tpu_custom_call" | custom-call | tf_op jit(solution)/shard_map/within/pallas_call | solution.py:476
  70.3 18.8 %norm.1.a_ref = bf16[512,4096]{1,0:T(8,128)(2,1)} custom-call(bf16[512,4096]{1,0:T(8,128)(2,1)} %get-tuple-element.18.y_ref, bf16[512,4096]{1,0:T(8,128)(2,1)} %gate_ref.1, bf16[512,512]{1,0:T(8,128)(2,1)} %get-tuple-element.14.mc_ref, f32[512,128]{1,0:T(8,128)} %get-tuple-element.16.rs_ref, bf16[3,8,128,512]{3,2,1,0:T(8,128)(2,1)} %get-tuple-element.19.enter_ref, ...), custom_call_target="tpu_custom_call" | custom-call | tf_op jit(solution)/shard_map/norm/pallas_call | solution.py:508
  89.1 34.6 %project.1 = bf16[128,4096]{1,0:T(8,128)(2,1)} custom-call(bf16[512,4096]{1,0:T(8,128)(2,1)} %norm.1.a_ref, bf16[4096,4096]{1,0:T(8,128)(2,1)} %w_ref.1), custom_call_target="tpu_custom_call" | custom-call | tf_op jit(solution)/shard_map/project/pallas_call | solution.py:536
  123.7 2.3 %copy.19 = bf16[128,4096]{1,0:T(8,128)(2,1)} copy(bf16[128,4096]{1,0:T(8,128)(2,1)} %project.1) | data formatting | bytes 2097152
  (2 shorter events, 0.0 us)
Async XLA Ops:
  1.6 8.9 %collective-permute-start = (bf16[8,4608]{1,0:T(8,128)(2,1)S(1)}, bf16[8,4608]{1,0:T(8,128)(2,1)S(1)}, u32[]{:S(2)}, u32[]{:S(2)}) collective-permute-start(bf16[8,4608]{1,0:T(8,128)(2,1)S(1)} %pad_maximum_fusion), channel_id=1, source_target_pairs={{0,4},{4,8},{8,12},{12,16},{16,20},{20,24},{24,28},{1,5},{5,9},{9,... | collective-permute-start | bytes 221192 | tf_op jit(solution)/shard_map/ppermute | solution.py:422
  10.4 0.6 copy-start

commit v2 on v1

v2 whole, which is shorter than its diff:
```python
import functools

import jax
import jax.numpy as jnp
from jax import lax
from jax.experimental import pallas as pl
from jax.experimental.pallas import tpu as pltpu
from jax.sharding import PartitionSpec as P

HEAD_DIM = 64
STATE = 128
CONV = 4
BLOCK = 128
WIDE = 512
LEAD = 16
TILE = 256
HEADS = 64
F32 = jnp.float32
BF16 = jnp.bfloat16
MESH = pl.DeviceIdType.MESH


def silu(v):
    half = 0.5 * v
    return half + half * jnp.tanh(half)


def dot(a, b):
    return jnp.dot(a, b, preferred_element_type=F32)


def two_parts(v):
    high = v.astype(BF16)
    low = (v - high.astype(F32)).astype(BF16)
    return jnp.concatenate([high, low], axis=1)


def spread_matrix(chunk, heads):
    rows = lax.broadcasted_iota(jnp.int32, (2 * heads, WIDE), 0)
    cols = lax.broadcasted_iota(jnp.int32, (2 * heads, WIDE), 1)
    rows = jnp.where(rows >= heads, rows - heads, rows)
    return jnp.where(rows == chunk * (WIDE // HEAD_DIM) + cols // HEAD_DIM, 1.0, 0.0).astype(BF16)


def conv_rows(padded, base, count, lanes, weights, bias):
    window = padded[pl.ds(base + LEAD - 8, count + 8), lanes]
    total = bias
    for tap in range(CONV):
        start = 8 - CONV + 1 + tap
        total = total + weights[tap] * window[start : start + count]
    return silu(total)


def mixer_kernel(
    pairs, start, x_ref, x_any, maps_ref, maps_any, cw_ref, cb_ref, mw_ref, mb_ref, step_ref,
    rate_ref, skip_ref, gate_ref, gain_ref, out_ref,
    padded, mpadded, lead_x, lead_m, load, tot, reach, prior, xc, mc, bt, rs, s_all, enter, y_all,
    inc, rolled, flipped, gated, square, mine, theirs, got, chain_in, chain_out, back_out,
    back_in, halo_send, halo_recv, log_send, log_recv, x_send, x_recv, c_send, c_recv, b_send,
    b_recv,
):
    i = pl.program_id(0)
    length = x_ref.shape[0]
    heads = rs.shape[1] // 2
    blocks = length // BLOCK
    groups = bt.shape[0]
    chunks = s_all.shape[0]
    per_half = chunks // 2
    per_group = chunks // groups
    half = 64
    place = lax.axis_index("ctx")
    pair, side = place // 2, place % 2
    first_pair, last_pair = pair == 0, pair == pairs - 1
    final = place == 2 * pairs - 1
    peer = {"ctx": pair * 2 + 1 - side}
    after_me, before_me = {"ctx": place + 1}, {"ctx": place - 1}
    ahead, behind = {"ctx": place + 2}, {"ctx": place - 2}

    def remote(src, dst, send, recv, target):
        return pltpu.make_async_remote_copy(
            src, dst, send, recv, device_id=target, device_id_type=MESH
        )

    def halo_copies():
        rows = pl.ds(length - LEAD, LEAD)
        return (
            remote(x_any.at[rows, :], lead_x, halo_send.at[0], halo_recv.at[0], after_me),
            remote(maps_any.at[rows, :], lead_m, halo_send.at[1], halo_recv.at[1], after_me),
        )

    def log_copy():
        return remote(mine, theirs, log_send, log_recv, peer)

    def x_copy(c):
        src = s_all.at[(1 - side) * per_half + c]
        return remote(src, got.at[c], x_send.at[c], x_recv.at[c], peer)

    def c_copy(c):
        return remote(chain_out.at[c], chain_in.at[c], c_send.at[c], c_recv.at[c], ahead)

    def b_copy(c):
        return remote(back_out.at[c], back_in.at[c], b_send.at[c], b_recv.at[c], peer)

    @pl.when(i == 0)
    def _():
        barrier = pltpu.get_barrier_semaphore()

        def greet(target):
            pl.semaphore_signal(barrier, inc=1, device_id=target, device_id_type=MESH)

        @pl.when(place > 0)
        def _():
            greet(before_me)

        @pl.when(jnp.logical_not(final))
        def _():
            greet(after_me)

        @pl.when(pair > 0)
        def _():
            greet(behind)

        @pl.when(jnp.logical_not(last_pair))
        def _():
            greet(ahead)

        count = (
            jnp.where(place > 0, 1, 0) + jnp.where(final, 0, 1)
            + jnp.where(pair > 0, 1, 0) + jnp.where(last_pair, 0, 1)
        )
        pl.semaphore_wait(barrier, count)

        @pl.when(jnp.logical_not(final))
        def _():
            for copy in halo_copies():
                copy.start()

        tri = (
            lax.broadcasted_iota(jnp.int32, (BLOCK, BLOCK), 0)
            >= lax.broadcasted_iota(jnp.int32, (BLOCK, BLOCK), 1)
        ).astype(F32)
        total = jnp.zeros((1, heads), F32)
        for b in range(blocks):
            rows = slice(b * BLOCK, (b + 1) * BLOCK)
            step = step_ref[:, rows].T
            running = jnp.dot(
                tri, -rate_ref[...] * step,
                precision=lax.Precision.HIGHEST, preferred_element_type=F32,
            )
            rs[rows] = jnp.concatenate([running, step], axis=1)
            last = running[BLOCK - 1 : BLOCK]
            load[rows] = two_parts(jnp.exp(last - running) * step)
            reach[rows] = two_parts(jnp.exp(running))
            tot[b] = jnp.broadcast_to(two_parts(jnp.exp(last)).astype(F32), (8, 2 * heads))
            prior[b] = jnp.broadcast_to(two_parts(jnp.exp(total)).astype(F32), (8, 2 * heads))
            total = total + last
        keep = jnp.exp(total)
        mine[...] = jnp.broadcast_to(jnp.concatenate([keep, keep], axis=1), (8, 2 * heads))
        log_copy().start()
        mpadded[LEAD:] = maps_ref[...].astype(F32)

        @pl.when(place == 0)
        def _():
            lead_x[...] = jnp.zeros_like(lead_x)
            lead_m[...] = jnp.zeros_like(lead_m)

        @pl.when(place > 0)
        def _():
            for copy in halo_copies():
                copy.wait_recv()

        mpadded[0:LEAD] = lead_m[...].astype(F32)
        width = groups * STATE
        for m in range(2):
            lanes = slice(m * width, (m + 1) * width)
            weights = [mw_ref[tap, m : m + 1] for tap in range(CONV)]
            for r in range(length // half):
                mapped = conv_rows(mpadded, r * half, half, lanes, weights, mb_ref[m : m + 1])
                mc[r * half : (r + 1) * half, lanes] = mapped.astype(BF16)
        for b in range(blocks):
            rows = slice(b * BLOCK, (b + 1) * BLOCK)
            for g in range(groups):
                own = mc[rows, g * STATE : (g + 1) * STATE].astype(F32)
                bt[g, :, rows] = own.T.astype(BF16)

    c = (i - 3 - 2 * pair) // 2

    @pl.when((c >= 0) & (c < per_half) & (i >= 3 + 2 * pair) & ((i - 3) % 2 == 0))
    def _():
        @pl.when(c == 0)
        def _():
            log_copy().wait_recv()

        x_copy(c).wait_recv()

        @pl.when(pair > 0)
        def _():
            c_copy(c).wait_recv()

        @pl.when(first_pair)
        def _():
            chain_in[c] = jnp.zeros_like(chain_in[c])

        spread = spread_matrix(side * per_half + c, heads)
        keep_mine = dot(two_parts(mine[:, 0:heads]), spread)[0:1]
        keep_theirs = dot(two_parts(theirs[:, 0:heads]), spread)[0:1]
        own = s_all[side * per_half + c].astype(F32)
        other = got[c].astype(F32)
        early = side == 0
        first = jnp.where(early, own, other)
        second = jnp.where(early, other, own)
        keep_first = jnp.where(early, keep_mine, keep_theirs)
        keep_second = jnp.where(early, keep_theirs, keep_mine)
        before = chain_in[c].astype(F32)
        middle = keep_first * before + first
        after = keep_second * middle + second
        back_out[c] = jnp.where(early, middle, before).astype(BF16)
        b_copy(c).start()

        @pl.when(jnp.logical_not(last_pair))
        def _():
            chain_out[c] = after.astype(BF16)
            c_copy(c).start()

        inc[side * per_half + c] = jnp.where(early, before, middle).astype(BF16)

    @pl.when(i < chunks)
    def _():
        chunk = (i % 2) * per_half + i // 2
        spread = spread_matrix(chunk, heads)
        lanes = pl.ds(pl.multiple_of(chunk * WIDE, WIDE), WIDE)
        padded[0:LEAD] = lead_x[:, lanes].astype(F32)

        def widen(r, _):
            at = pl.multiple_of(r * half, half)
            padded[pl.ds(at + LEAD, half), :] = x_ref[pl.ds(at, half), :].astype(F32)
            return 0

        lax.fori_loop(0, length // half, widen, 0)
        weights, bias = [cw_ref[tap : tap + 1] for tap in range(CONV)], cb_ref[...]

        def conv(r, _):
            at = pl.multiple_of(r * half, half)
            done = conv_rows(padded, at, half, slice(None), weights, bias)
            xc[chunk, pl.ds(at, half), :] = done.astype(BF16)
            return 0

        lax.fori_loop(0, length // half, conv, 0)
        group = chunk // per_group
        state = jnp.zeros((STATE, WIDE), F32)
        for b in range(blocks):
            rows = slice(b * BLOCK, (b + 1) * BLOCK)
            if b > 0:
                enter[b - 1, chunk] = state.astype(BF16)
            scaled = (xc[chunk, rows].astype(F32) * dot(load[rows], spread)).astype(BF16)
            fresh = dot(bt[group, :, rows], scaled)
            if b > 0:
                keep = dot(tot[b].astype(BF16), spread)[0:1]
                state = keep * state + fresh
            else:
                state = fresh
        s_all[chunk] = state.astype(BF16)

        @pl.when(i % 2 == 1)
        def _():
            x_copy(i // 2).start()

    @pl.when((i >= chunks) & (i < 2 * chunks))
    def _():
        chunk = i - chunks
        per = WIDE // HEAD_DIM
        wide = pltpu.roll(rs[...], (2 * heads - chunk * per) % (2 * heads), 1)
        rolled[...] = wide
        turned = wide.T
        flipped[...] = turned[0:per] - jnp.log(turned[heads : heads + per])
        group = chunk // per_group

        def block(b, _):
            at = pl.multiple_of(b * BLOCK, BLOCK)
            rows = pl.ds(at, BLOCK)
            out_map = mc[rows, pl.ds(pl.multiple_of((groups + group) * STATE, STATE), STATE)]
            score = dot(out_map, bt[group, :, rows])
            causal = (
                lax.broadcasted_iota(jnp.int32, (BLOCK, BLOCK), 0)
                >= lax.broadcasted_iota(jnp.int32, (BLOCK, BLOCK), 1)
            )
            score = jnp.where(causal, score, 0.0)
            lower = lax.broadcasted_iota(jnp.int32, (BLOCK, 2 * HEAD_DIM), 1) < HEAD_DIM
            columns = rolled[rows, :]
            for p in range(WIDE // (2 * HEAD_DIM)):
                parts = []
                for h in (2 * p, 2 * p + 1):
                    gap = columns[:, h : h + 1] - flipped[h : h + 1, rows]
                    decay = jnp.exp(jnp.where(causal, gap, -1e30))
                    parts.append((score * decay).astype(BF16))
                lanes = slice(p * 2 * HEAD_DIM, (p + 1) * 2 * HEAD_DIM)
                x = xc[chunk, rows, lanes]
                zero = jnp.zeros_like(x)
                both = jnp.concatenate([jnp.where(lower, x, zero), jnp.where(lower, zero, x)], axis=0)
                y = dot(jnp.concatenate(parts, axis=1), both)
                y_all[chunk, rows, lanes] = (y + skip_ref[:, lanes] * x.astype(F32)).astype(BF16)
            return 0

        lax.fori_loop(0, blocks, block, 0)

    @pl.when(i == start)
    def _():
        log_copy().wait_send()

        @pl.when(jnp.logical_not(final))
        def _():
            for copy in halo_copies():
                copy.wait_send()

        def finish(c, _):
            x_copy(c).wait_send()
            b_copy(c).wait_send()
            b_copy(c).wait_recv()
            inc[(1 - side) * per_half + c] = back_in[c]

            @pl.when(jnp.logical_not(last_pair))
            def _():
                c_copy(c).wait_send()

            return 0

        lax.fori_loop(0, per_half, finish, 0)

    @pl.when(i >= start)
    def _():
        chunk = i - start
        group, j = chunk // per_group, chunk % per_group
        spread = spread_matrix(chunk, heads)
        map_lanes = pl.ds(pl.multiple_of((groups + group) * STATE, STATE), STATE)
        for b in range(blocks):
            rows = slice(b * BLOCK, (b + 1) * BLOCK)
            incoming = inc[chunk].astype(F32)
            if b > 0:
                keep = dot(prior[b].astype(BF16), spread)[0:1]
                incoming = keep * incoming + enter[b - 1, chunk].astype(F32)
            before = dot(mc[rows, map_lanes], incoming.astype(BF16))
            value = y_all[chunk, rows].astype(F32) + dot(reach[rows], spread) * before
            value = value * silu(gate_ref[rows].astype(F32))
            gated[j, rows] = value
            part = jnp.sum(value * value, axis=1, keepdims=True)
            part = jnp.broadcast_to(part, (BLOCK, 128))

            @pl.when(j == 0)
            def _():
                square[rows] = part

            @pl.when(j > 0)
            def _():
                square[rows] = square[rows] + part

        @pl.when(j == per_group - 1)
        def _():
            for b in range(blocks):
                rows = slice(b * BLOCK, (b + 1) * BLOCK)
                mean = square[rows][:, 0:1] * (1.0 / (per_group * WIDE))
                inverse = lax.rsqrt(mean + 1e-05)
                for k in range(out_ref.shape[1] // WIDE):
                    lanes = slice(k * WIDE, (k + 1) * WIDE)
                    scaled = gated[k, rows] * inverse * gain_ref[:, lanes]
                    out_ref[rows, lanes] = scaled.astype(BF16)


def project_kernel(
    tiles, fars, a_ref, w_ref, o_ref, part, send, recv, hop_keep, hop_send, hop_recv,
    s_send, s_recv, h_send, h_recv,
):
    i = pl.program_id(0)
    place = lax.axis_index("tp")
    far, core = place // 2, place % 2
    peer = {"tp": far * 2 + 1 - core}
    share = o_ref.shape[0]

    def across(d):
        return {"tp": (far + d) % fars * 2 + core}

    def near_copy(t):
        return pltpu.make_async_remote_copy(
            send.at[t], recv.at[t], s_send.at[t], s_recv.at[t],
            device_id=peer, device_id_type=MESH,
        )

    def far_copy(t, d):
        at = t * (fars - 1) + d - 1
        return pltpu.make_async_remote_copy(
            hop_send.at[at], hop_recv.at[at], h_send.at[at], h_recv.at[at],
            device_id=across(d), device_id_type=MESH,
        )

    @pl.when(i == 0)
    def _():
        barrier = pltpu.get_barrier_semaphore()
        pl.semaphore_signal(barrier, inc=1, device_id=peer, device_id_type=MESH)
        for d in range(1, fars):
            pl.semaphore_signal(barrier, inc=1, device_id=across(d), device_id_type=MESH)
        pl.semaphore_wait(barrier, fars)

    @pl.when(i < tiles)
    def _():
        part[i % 2] = dot(a_ref[...], w_ref[...])
        for q in range(fars):
            theirs = pl.multiple_of((q * 2 + 1 - core) * share, share)
            send[i, q] = part[i % 2, pl.ds(theirs, share), :].astype(BF16)
        near_copy(i).start()

    @pl.when((i >= 1) & (i < tiles + 1))
    def _():
        t = i - 1
        near_copy(t).wait_recv()
        for d in range(1, fars):
            q = (far + d) % fars
            own = pl.multiple_of((q * 2 + core) * share, share)
            total = part[t % 2, pl.ds(own, share), :] + recv[t, q].astype(F32)
            hop_send[t * (fars - 1) + d - 1] = total.astype(BF16)
            far_copy(t, d).start()
        own = pl.multiple_of((far * 2 + core) * share, share)
        hop_keep[t] = part[t % 2, pl.ds(own, share), :] + recv[t, far].astype(F32)

    @pl.when(i >= 3)
    def _():
        t = i - 3
        total = hop_keep[t]
        for d in range(1, fars):
            far_copy(t, d).wait_recv()
            total = total + hop_recv[t * (fars - 1) + d - 1].astype(F32)
        o_ref[...] = total.astype(BF16)
        near_copy(t).wait_send()
        for d in range(1, fars):
            far_copy(t, d).wait_send()


def whole(shape):
    return pl.BlockSpec(shape, lambda *_: (0,) * len(shape))


def local(
    ctx_size, tp_size, ssm_input, gate_input, state_maps, step_size, decay_rate, skip_gain, conv_weight,
    conv_bias, map_conv, map_bias, norm_gain, out_weight,
):
    length, width = ssm_input.shape
    steps_t = jnp.pad(step_size.T, ((0, HEADS - step_size.shape[1]), (0, 0)))
    decay_rate = jnp.pad(decay_rate, (0, HEADS - decay_rate.shape[0]))
    heads = HEADS
    groups = state_maps.shape[2] // STATE
    blocks = length // BLOCK
    chunks = width // WIDE
    per_half = chunks // 2
    per_group = chunks // groups
    group_width = width // groups
    maps_width = 2 * groups * STATE
    maps = state_maps.reshape(length, maps_width)
    pairs = ctx_size // 2
    start = max(2 * chunks, 2 * (per_half - 1) + 4 + 2 * (pairs - 1))
    shape = jax.ShapeDtypeStruct
    dma = pltpu.SemaphoreType.DMA
    vmem = pltpu.VMEM

    def early(i):
        i = jnp.minimum(i, chunks - 1)
        return (0, (i % 2) * per_half + i // 2)

    def inner(i):
        return (0, jnp.clip(i - chunks, 0, chunks - 1))

    def late(i):
        return (0, jnp.clip(i - start, 0, chunks - 1))

    def late_group(i):
        return (0, jnp.clip(i - start, 0, chunks - 1) // per_group)

    slab = vmem((per_half, STATE, WIDE), BF16)
    normed = pl.pallas_call(
        functools.partial(mixer_kernel, pairs, start),
        grid=(start + chunks,),
        in_specs=[
            pl.BlockSpec((length, WIDE), early),
            pl.BlockSpec(memory_space=pl.ANY),
            whole((length, maps_width)),
            pl.BlockSpec(memory_space=pl.ANY),
            pl.BlockSpec((CONV, WIDE), early),
            pl.BlockSpec((1, WIDE), early),
            whole(map_conv.shape),
            whole(map_bias.shape),
            whole((heads, length)),
            whole((1, heads)),
            pl.BlockSpec((1, WIDE), inner),
            pl.BlockSpec((length, WIDE), late),
            pl.BlockSpec((1, group_width), late_group),
        ],
        out_specs=pl.BlockSpec((length, group_width), late_group),
        out_shape=shape((length, width), BF16),
        scratch_shapes=[
            vmem((length + LEAD, WIDE), F32),
            vmem((length + LEAD, maps_width), F32),
            vmem((LEAD, width), BF16),
            vmem((LEAD, maps_width), BF16),
            vmem((length, 2 * heads), BF16),
            vmem((blocks, 8, 2 * heads), F32),
            vmem((length, 2 * heads), BF16),
            vmem((blocks, 8, 2 * heads), F32),
            vmem((chunks, length, WIDE), BF16),
            vmem((length, maps_width), BF16),
            vmem((groups, STATE, length), BF16),
            vmem((length, 2 * heads), F32),
            vmem((chunks, STATE, WIDE), BF16),
            vmem((blocks - 1, chunks, STATE, WIDE), BF16),
            vmem((chunks, length, WIDE), BF16),
            vmem((chunks, STATE, WIDE), BF16),
            vmem((length, 2 * heads), F32),
            vmem((WIDE // HEAD_DIM, length), F32),
            vmem((per_group, length, WIDE), F32),
            vmem((length, 128), F32),
            vmem((8, 2 * heads), F32),
            vmem((8, 2 * heads), F32),
            slab, slab, slab, slab, slab,
            dma((2,)), dma((2,)), dma, dma,
        ] + [dma((per_half,))] * 6,
        compiler_params=pltpu.CompilerParams(
            collective_id=0, has_side_effects=True, vmem_limit_bytes=56 * 1024 * 1024
        ),
        name="mixer",
    )(
        ssm_input, ssm_input, maps, maps, conv_weight, conv_bias[None], map_conv, map_bias,
        steps_t, decay_rate[None], jnp.repeat(skip_gain, HEAD_DIM)[None], gate_input,
        norm_gain[None],
    )
    d_out = out_weight.shape[1]
    tiles = d_out // TILE
    share = length // tp_size
    fars = tp_size // 2
    hops = tiles * (fars - 1)
    return pl.pallas_call(
        functools.partial(project_kernel, tiles, fars),
        grid=(tiles + 3,),
        in_specs=[
            whole((length, width)),
            pl.BlockSpec((width, TILE), lambda i: (0, jnp.minimum(i, tiles - 1))),
        ],
        out_specs=pl.BlockSpec((share, TILE), lambda i: (0, jnp.maximum(i - 3, 0))),
        out_shape=shape((share, d_out), BF16),
        scratch_shapes=[
            pltpu.VMEM((2, length, TILE), F32),
            pltpu.VMEM((tiles, fars, share, TILE), BF16),
            pltpu.VMEM((tiles, fars, share, TILE), BF16),
            pltpu.VMEM((tiles, share, TILE), F32),
            pltpu.VMEM((hops, share, TILE), BF16),
            pltpu.VMEM((hops, share, TILE), BF16),
        ] + [dma((tiles,))] * 2 + [dma((hops,))] * 2,
        compiler_params=pltpu.CompilerParams(
            collective_id=1, has_side_effects=True, vmem_limit_bytes=56 * 1024 * 1024
        ),
        name="project",
    )(normed, out_weight)


def solution(mesh):
    in_specs = (
        P("ctx", "tp"), P("ctx", "tp"), P("ctx", None, "tp"), P("ctx", "tp"), P("tp"), P("tp"),
        P(None, "tp"), P("tp"), P(None, None, "tp"), P(None, "tp"), P("tp"), P("tp", None),
    )
    return jax.shard_map(
        functools.partial(local, mesh.shape["ctx"], mesh.shape["tp"]), mesh=mesh, in_specs=in_specs,
        out_specs=P(("ctx", "tp"), None), check_vma=False,
    )
```

time: 126 us -> 112 us (0.89); the launches traced: 126 us -> 110 us
  Pallas kernels: 113 us -> 104 us
  local copies, waits for them, and re-layouts: 12 us -> 5.62 us
  starting transfers between devices: 1.29 us -> 0 us
    pallas_call x3 -> x1, Pallas kernels: 78 us -> 69.3 us  [local(): pl.pallas_call(functools.partial(mixer_kernel, pairs, start), grid=(start...]
    unnamed x9 -> x2, local copies, waits for them, and re-layouts: 9.78 us -> 4.21 us
    ppermute x1 -> x0, starting transfers between devices: 1.29 us -> none  [local(): lead = lax.ppermute(tail, 'ctx', [(k, k + 1) for k in range(ctx_size - 1)])]
  transfers between devices with their start and end apart: 1 -> 0, of which waited for: 0 -> 0; matrix products, arithmetic and copies ran while one was open for 6% -> 0% of each run, Pallas kernels for 0% -> 0%
where the time goes in v2:
time: 112 us; the launch traced here: 110 us
  Pallas kernels  104 us (93%)
  local copies, waits for them, and re-layouts  5.62 us (5%)
    pallas_call x1, Pallas kernels, local(): pl.pallas_call(functools.partial(mixer_kernel, pairs, start), grid=(start...  69.3 us
    pallas_call x1, Pallas kernels, local(): pl.pallas_call(functools.partial(project_kernel, tiles, fars), grid=(tile...  34.9 us
    unnamed x2, local copies, waits for them, and re-layouts  4.21 us

profile of v2, /device:TPU:26, one launch (start us, length us, event | category | flops | bytes accessed | tf_op | source)
XLA Modules:
  0.0 109.8 jit_solution(25245050696249435)
XLA Ops:
  0.0 0.7 broadcast_in_dim.14
  0.7 0.7 broadcast_in_dim_reshape.3.skip_ref
  1.4 1.9 %copy.13 = bf16[64,8,2,256]{3,1,2,0:T(8,128)(2,1)} copy(bf16[64,8,2,256]{3,2,1,0:T(2,128)(2,1)} %bitcast.8) | data formatting | bytes 1048576
  3.3 69.3 %mixer.1.a_ref = bf16[512,4096]{1,0:T(8,128)(2,1)} custom-call(bf16[512,4096]{1,0:T(8,128)(2,1)} %x_any.1, bf16[512,4096]{1,0:T(8,128)(2,1)} %x_any.1, bf16[512,512]{1,0:T(8,128)(2,1)} %bitcast.6, bf16[512,512]{1,0:T(8,128)(2,1)} %bitcast.7, f32[4,4096]{1,0:T(4,128)} %cw_ref.1, f32[1,4096]{1,0:T(1,128)} %bitcast.10, f32[4,2,256]{2,1,0:T(2,128)} %mw_ref.1, ...), custom_call_target="tpu_custom_call" | custom-call | tf_op jit(solution)/shard_map/mixer/pallas_call | solution.py:476
  72.6 34.9 %project.1 = bf16[128,4096]{1,0:T(8,128)(2,1)} custom-call(bf16[512,4096]{1,0:T(8,128)(2,1)} %mixer.1.a_ref, bf16[4096,4096]{1,0:T(8,128)(2,1)} %w_ref.1), custom_call_target="tpu_custom_call" | custom-call | tf_op jit(solution)/shard_map/project/pallas_call | solution.py:536
  107.5 2.3 %copy.15 = bf16[128,4096]{1,0:T(8,128)(2,1)} copy(bf16[128,4096]{1,0:T(8,128)(2,1)} %project.1) | data formatting | bytes 2097152

commit v3 on v2

--- a/solution.py
+++ b/solution.py
@@ -14,6 +14,7 @@
 WIDE = 512
 LEAD = 16
 TILE = 256
+NARROW = 256
 HEADS = 64
 F32 = jnp.float32
 BF16 = jnp.bfloat16
@@ -42,19 +43,22 @@
     return jnp.where(rows == chunk * (WIDE // HEAD_DIM) + cols // HEAD_DIM, 1.0, 0.0).astype(BF16)
 
 
-def conv_rows(padded, base, count, lanes, weights, bias):
-    window = padded[pl.ds(base + LEAD - 8, count + 8), lanes]
+def conv_window(window, count, weights, bias):
     total = bias
     for tap in range(CONV):
-        start = 8 - CONV + 1 + tap
+        start = LEAD - CONV + 1 + tap
         total = total + weights[tap] * window[start : start + count]
     return silu(total)
+
+
+def conv_rows(padded, base, count, lanes, weights, bias):
+    return conv_window(padded[pl.ds(base, count + LEAD), lanes], count, weights, bias)
 
 
 def mixer_kernel(
     pairs, start, x_ref, x_any, maps_ref, maps_any, cw_ref, cb_ref, mw_ref, mb_ref, step_ref,
     rate_ref, skip_ref, gate_ref, gain_ref, out_ref,
-    padded, mpadded, lead_x, lead_m, load, tot, reach, prior, xc, mc, bt, rs, s_all, enter, y_all,
+    mpadded, lead_x, lead_m, load, tot, reach, prior, xc, mc, bt, rs, s_all, enter, y_all,
     inc, rolled, flipped, gated, square, mine, theirs, got, chain_in, chain_out, back_out,
     back_in, halo_send, halo_recv, log_send, log_recv, x_send, x_recv, c_send, c_recv, b_send,
     b_recv,
@@ -228,38 +232,36 @@
     def _():
         chunk = (i % 2) * per_half + i // 2
         spread = spread_matrix(chunk, heads)
-        lanes = pl.ds(pl.multiple_of(chunk * WIDE, WIDE), WIDE)
-        padded[0:LEAD] = lead_x[:, lanes].astype(F32)
-
-        def widen(r, _):
-            at = pl.multiple_of(r * half, half)
-            padded[pl.ds(at + LEAD, half), :] = x_ref[pl.ds(at, half), :].astype(F32)
-            return 0
-
-        lax.fori_loop(0, length // half, widen, 0)
-        weights, bias = [cw_ref[tap : tap + 1] for tap in range(CONV)], cb_ref[...]
-
-        def conv(r, _):
-            at = pl.multiple_of(r * half, half)
-            done = conv_rows(padded, at, half, slice(None), weights, bias)
-            xc[chunk, pl.ds(at, half), :] = done.astype(BF16)
-            return 0
-
-        lax.fori_loop(0, length // half, conv, 0)
         group = chunk // per_group
-        state = jnp.zeros((STATE, WIDE), F32)
-        for b in range(blocks):
-            rows = slice(b * BLOCK, (b + 1) * BLOCK)
-            if b > 0:
-                enter[b - 1, chunk] = state.astype(BF16)
-            scaled = (xc[chunk, rows].astype(F32) * dot(load[rows], spread)).astype(BF16)
-            fresh = dot(bt[group, :, rows], scaled)
-            if b > 0:
-                keep = dot(tot[b].astype(BF16), spread)[0:1]
-                state = keep * state + fresh
-            else:
-                state = fresh
-        s_all[chunk] = state.astype(BF16)
+        for low in range(0, WIDE, NARROW):
+            lanes = slice(low, low + NARROW)
+            lead_lanes = pl.ds(pl.multiple_of(chunk * WIDE + low, NARROW), NARROW)
+            weights = [cw_ref[tap : tap + 1, lanes] for tap in range(CONV)]
+            bias = cb_ref[:, lanes]
+            for r in range(length // half):
+                at = r * half
+                if r == 0:
+                    window = jnp.concatenate(
+                        [lead_x[:, lead_lanes].astype(F32), x_ref[0:half, lanes].astype(F32)], axis=0
+                    )
+                else:
+                    window = x_ref[at - LEAD : at + half, lanes].astype(F32)
+                done = conv_window(window, half, weights, bias)
+                xc[chunk, at : at + half, lanes] = done.astype(BF16)
+            state = jnp.zeros((STATE, NARROW), F32)
+            for b in range(blocks):
+                rows = slice(b * BLOCK, (b + 1) * BLOCK)
+                if b > 0:
+                    enter[b - 1, chunk, :, lanes] = state.astype(BF16)
+                factor = dot(load[rows], spread[:, lanes])
+                scaled = (xc[chunk, rows, lanes].astype(F32) * factor).astype(BF16)
+                fresh = dot(bt[group, :, rows], scaled)
+                if b > 0:
+                    keep = dot(tot[b].astype(BF16), spread[:, lanes])[0:1]
+                    state = keep * state + fresh
+                else:
+                    state = fresh
+            s_all[chunk, :, lanes] = state.astype(BF16)
 
         @pl.when(i % 2 == 1)
         def _():
@@ -301,10 +303,11 @@
                 y_all[chunk, rows, lanes] = (y + skip_ref[:, lanes] * x.astype(F32)).astype(BF16)
             return 0
 
-        lax.fori_loop(0, blocks, block, 0)
+        lax.fori_loop(0, blocks, block, 0, unroll=True)
 
     @pl.when(i == start)
     def _():
+        square[...] = jnp.zeros_like(square)
         log_copy().wait_send()
 
         @pl.when(jnp.logical_not(final))
@@ -334,35 +337,34 @@
         map_lanes = pl.ds(pl.multiple_of((groups + group) * STATE, STATE), STATE)
         for b in range(blocks):
             rows = slice(b * BLOCK, (b + 1) * BLOCK)
-            incoming = inc[chunk].astype(F32)
-            if b > 0:
-                keep = dot(prior[b].astype(BF16), spread)[0:1]
-                incoming = keep * incoming + enter[b - 1, chunk].astype(F32)
-            before = dot(mc[rows, map_lanes], incoming.astype(BF16))
-            value = y_all[chunk, rows].astype(F32) + dot(reach[rows], spread) * before
-            value = value * silu(gate_ref[rows].astype(F32))
-            gated[j, rows] = value
-            part = jnp.sum(value * value, axis=1, keepdims=True)
-            part = jnp.broadcast_to(part, (BLOCK, 128))
-
-            @pl.when(j == 0)
-            def _():
-                square[rows] = part
-
-            @pl.when(j > 0)
-            def _():
-                square[rows] = square[rows] + part
+            part = square[rows]
+            for low in range(0, WIDE, NARROW):
+                lanes = slice(low, low + NARROW)
+                incoming = inc[chunk, :, lanes].astype(F32)
+                if b > 0:
+                    keep = dot(prior[b].astype(BF16), spread[:, lanes])[0:1]
+                    incoming = keep * incoming + enter[b - 1, chunk, :, lanes].astype(F32)
+                before = dot(mc[rows, map_lanes], incoming.astype(BF16))
+                reached = dot(reach[rows], spread[:, lanes])
+                value = y_all[chunk, rows, lanes].astype(F32) + reached * before
+                value = value * silu(gate_ref[rows, lanes].astype(F32))
+                gated[j, rows, lanes] = value
+                power = value * value
+                for k in range(NARROW // 128):
+                    part = part + power[:, k * 128 : (k + 1) * 128]
+            square[rows] = part
 
         @pl.when(j == per_group - 1)
         def _():
             for b in range(blocks):
                 rows = slice(b * BLOCK, (b + 1) * BLOCK)
-                mean = square[rows][:, 0:1] * (1.0 / (per_group * WIDE))
+                mean = jnp.sum(square[rows], axis=1, keepdims=True) * (1.0 / (per_group * WIDE))
                 inverse = lax.rsqrt(mean + 1e-05)
                 for k in range(out_ref.shape[1] // WIDE):
                     lanes = slice(k * WIDE, (k + 1) * WIDE)
                     scaled = gated[k, rows] * inverse * gain_ref[:, lanes]
                     out_ref[rows, lanes] = scaled.astype(BF16)
+                square[rows] = jnp.zeros((BLOCK, 128), F32)
 
 
 def project_kernel(
@@ -494,7 +496,6 @@
         out_specs=pl.BlockSpec((length, group_width), late_group),
         out_shape=shape((length, width), BF16),
         scratch_shapes=[
-            vmem((length + LEAD, WIDE), F32),
             vmem((length + LEAD, maps_width), F32),
             vmem((LEAD, width), BF16),
             vmem((LEAD, maps_width), BF16),

time: 112 us -> 108 us (0.964); the launches traced: 110 us -> 107 us
  Pallas kernels: 104 us -> 101 us
    pallas_call x1, Pallas kernels: 69.3 us -> 66.5 us  [local(): pl.pallas_call(functools.partial(mixer_kernel, pairs, start), grid=(start...]
where the time goes in v3:
time: 108 us; the launch traced here: 107 us
  Pallas kernels  101 us (94%)
  local copies, waits for them, and re-layouts  5.62 us (5%)
    pallas_call x1, Pallas kernels, local(): pl.pallas_call(functools.partial(mixer_kernel, pairs, start), grid=(start...  66.5 us
    pallas_call x1, Pallas kernels, local(): pl.pallas_call(functools.partial(project_kernel, tiles, fars), grid=(tile...  34.9 us
    unnamed x2, local copies, waits for them, and re-layouts  4.21 us

profile of v3, /device:TPU:26, one launch (start us, length us, event | category | flops | bytes accessed | tf_op | source)
XLA Modules:
  0.0 107.1 jit_solution(13835678048218820517)
XLA Ops:
  0.0 0.7 broadcast_in_dim.14
  0.7 0.7 broadcast_in_dim_reshape.3.skip_ref
  1.4 1.9 %copy.13 = bf16[64,8,2,256]{3,1,2,0:T(8,128)(2,1)} copy(bf16[64,8,2,256]{3,2,1,0:T(2,128)(2,1)} %bitcast.8) | data formatting | bytes 1048576
  3.3 66.5 %mixer.1.a_ref = bf16[512,4096]{1,0:T(8,128)(2,1)} custom-call(bf16[512,4096]{1,0:T(8,128)(2,1)} %x_any.1, bf16[512,4096]{1,0:T(8,128)(2,1)} %x_any.1, bf16[512,512]{1,0:T(8,128)(2,1)} %bitcast.6, bf16[512,512]{1,0:T(8,128)(2,1)} %bitcast.7, f32[4,4096]{1,0:T(4,128)} %cw_ref.1, f32[1,4096]{1,0:T(1,128)} %bitcast.10, f32[4,2,256]{2,1,0:T(2,128)} %mw_ref.1, ...), custom_call_target="tpu_custom_call" | custom-call | tf_op jit(solution)/shard_map/mixer/pallas_call | solution.py:478
  69.9 34.9 %project.1 = bf16[128,4096]{1,0:T(8,128)(2,1)} custom-call(bf16[512,4096]{1,0:T(8,128)(2,1)} %mixer.1.a_ref, bf16[4096,4096]{1,0:T(8,128)(2,1)} %w_ref.1), custom_call_target="tpu_custom_call" | custom-call | tf_op jit(solution)/shard_map/project/pallas_call | solution.py:537
  104.8 2.3 %copy.15 = bf16[128,4096]{1,0:T(8,128)(2,1)} copy(bf16[128,4096]{1,0:T(8,128)(2,1)} %project.1) | data formatting | bytes 2097152
